TPU v7x, 32 devices: a whole 2x2x4 slice. The times are simulated.
32 devices in a mesh: groups: 2 (over y), rows: 4 (over z), section: 2 (over x), feat: 2 (over core).
Axes of the slice: x: 2, y: 2, z: 4, core: 2. Of those that a mesh axis runs over, the one named last changes fastest.
Arguments:
- test_rows: bfloat16 [3, 256, 8, 512], P(None, ('groups', 'rows'), 'feat'), parts along dimension 1, may hold values from -6 to 6
- train_cache: bfloat16 [2, 2, 32, 8, 512], P('section', None, ('groups', 'rows'), 'feat'), parts along dimension 2, may hold values from -6 to 6
- pattern: int32 [8, 8], replicated, may hold values 0 or 1
- feat_qkv: bfloat16 [2, 512, 1536], P('section'), may hold values from -0.25 to 0.25
- feat_out: bfloat16 [2, 512, 512], P('section'), may hold values from -0.25 to 0.25
- item_query: bfloat16 [2, 512, 512], P('section'), may hold values from -0.25 to 0.25
- item_out: bfloat16 [2, 512, 512], P('section'), may hold values from -0.25 to 0.25
- gains: float32 [2, 2, 512], P('section'), may hold values from 0.5 to 1.5
Outputs:
- hidden: bfloat16 [2, 3, 256, 8, 512], P('section', None, ('groups', 'rows'), 'feat'), parts along dimension 2
There are 2 independent parts, one for each index of `groups`. A program takes and returns all parts, laid end to end along the dimension named above; an argument that names none is the same for every part. Nothing has to cross between parts.
All inputs are finite; a program needn't handle non-finite values.
Results may differ from a plain program's by a relative error of at most 0.02.
Values may be sent and summed in bfloat16 or wider, within the bound.
A program may use at most 64 MiB of HBM per device.

v0:
```python
import jax
import jax.numpy as jnp
from jax import lax
from jax.sharding import PartitionSpec as P

HEADS = 8


HIGH = lax.Precision.HIGHEST


def from_behind(block, axis, distance):
    devices = range(lax.axis_size(axis))
    route = [(i - distance, i) for i in devices if i - distance in devices]
    return lax.ppermute(block, axis, route)


def normed(x, gain):
    mean_sq = jnp.mean(x * x, axis=-1, keepdims=True)
    return x * lax.rsqrt(mean_sq + 1e-06) * gain


def per_device(test_rows, train_cache, pattern, feat_qkv, feat_out, item_query, item_out, gains):
    micro, test_n, group_dev, width = test_rows.shape
    heads = HEADS
    head_dim = width // heads
    scale = 1.0 / head_dim**0.5
    section = lax.axis_index("section")
    sections = lax.axis_size("section")
    feat_index = lax.axis_index("feat")
    groups = group_dev * lax.axis_size("feat")
    wqkv = feat_qkv[0]
    wout = feat_out[0]
    wquery = item_query[0]
    witem = item_out[0]
    gain_a = gains[0, 0]
    gain_b = gains[0, 1]
    mine = feat_index * group_dev + jnp.arange(group_dev)
    every = jnp.arange(groups)
    pattern_rows = lax.dynamic_slice_in_dim(pattern, feat_index * group_dev, group_dev, 0)
    allowed = (pattern_rows != 0) | (mine[:, None] == every[None, :])
    cache = train_cache[0]
    buffer = jnp.zeros((micro, test_n, group_dev, width), jnp.bfloat16)
    passed = jnp.zeros((test_n, group_dev, width), jnp.bfloat16)
    ticks = micro + sections - 1
    for tick in range(ticks):
        entering = test_rows[min(tick, micro - 1)]
        current = jnp.where(section == 0, entering, passed).astype(jnp.float32)
        a_local = normed(current, gain_a).astype(jnp.bfloat16)
        flat = a_local.reshape(test_n * group_dev, width)
        qkv = jnp.dot(flat, wqkv, preferred_element_type=jnp.float32).astype(jnp.bfloat16)
        qkv = qkv.reshape(test_n, group_dev, 3 * width)
        query = qkv[:, :, :width]
        pairs = lax.all_gather(qkv[:, :, width:], "feat", axis=1, tiled=True)
        query = query.reshape(test_n, group_dev, heads, head_dim)
        keys = pairs[:, :, :width].reshape(test_n, groups, heads, head_dim)
        values = pairs[:, :, width:].reshape(test_n, groups, heads, head_dim)
        scores = (
            jnp.einsum("rihd,rjhd->rhij", query, keys, preferred_element_type=jnp.float32) * scale
        )
        scores = jnp.where(allowed[None, None], scores, -1e30)
        weights = jax.nn.softmax(scores, axis=-1).astype(jnp.bfloat16)
        mixed = jnp.einsum(
            "rhij,rjhd->rihd", weights, values, preferred_element_type=jnp.float32
        ).astype(jnp.bfloat16)
        feature_term = jnp.dot(
            mixed.reshape(test_n * group_dev, width), wout, preferred_element_type=jnp.float32
        )
        h1 = current + feature_term.reshape(test_n, group_dev, width)
        b_local = normed(h1, gain_b).astype(jnp.bfloat16).reshape(test_n * group_dev, width)
        item_q = jnp.dot(b_local, wquery, preferred_element_type=jnp.float32).astype(jnp.bfloat16)
        item_q = item_q.reshape(test_n, group_dev, heads, head_dim)
        start_top = jnp.full((test_n, group_dev, heads), -1e30, jnp.float32)
        piece = lax.all_gather(cache, "rows", axis=1, tiled=True)
        top = start_top
        count = piece.shape[1]
        piece_k = piece[0].reshape(count, group_dev, heads, head_dim)
        piece_v = piece[1].astype(jnp.float32).reshape(count, group_dev, heads, head_dim)
        item_s = (
            jnp.einsum("rghd,nghd->rghn", item_q, piece_k, preferred_element_type=jnp.float32)
            * scale
        )
        new_top = jnp.maximum(top, jnp.max(item_s, axis=-1))
        expo = jnp.exp(item_s - new_top[..., None])
        total = jnp.sum(expo, axis=-1)
        accum = jnp.einsum("rghn,nghd->rghd", expo, piece_v, precision=HIGH)
        top, total, accum = (new_top, total, accum)
        item_mix = accum / total[..., None]
        item_mix = item_mix.astype(jnp.bfloat16).reshape(test_n * group_dev, width)
        term = jnp.dot(item_mix, witem, preferred_element_type=jnp.float32)
        result = (h1 + term.reshape(test_n, group_dev, width)).astype(jnp.bfloat16)
        slot = tick - section
        valid = (slot >= 0) & (slot < micro)
        place = jnp.clip(slot, 0, micro - 1)
        older = lax.dynamic_index_in_dim(buffer, place, 0, keepdims=False)
        buffer = lax.dynamic_update_index_in_dim(buffer, jnp.where(valid, result, older), place, 0)
        if tick + 1 < ticks:
            passed = from_behind(result, "section", 1)
    return buffer[None]


def solution(mesh):
    return jax.shard_map(
        per_device,
        mesh=mesh,
        in_specs=(
            P(None, ("groups", "rows"), "feat", None),
            P("section", None, ("groups", "rows"), "feat", None),
            P(),
            P("section", None, None),
            P("section", None, None),
            P("section", None, None),
            P("section", None, None),
            P("section", None, None),
        ),
        out_specs=P("section", None, ("groups", "rows"), "feat", None),
        check_vma=False,
    )
```

profile of v0, /device:TPU:3, one launch (start us, length us, event | category | flops | bytes accessed | tf_op | source)
XLA Modules:
  0.0 147.0 jit_solution(2902149152831472718)
XLA Ops:
  0.0 2.0 %fusion.112 = (bf16[1,32,4,512]{3,2,1,0:T(4,128)(2,1)}, bf16[1,32,4,512]{3,2,1,0:T(4,128)(2,1)}, bf16[1,32,4,512]{3,2,1,0:T(4,128)(2,1)S(1)}) fusion(bf16[3,32,4,512]{3,2,1,0:T(4,128)(2,1)} %param.8), kind=kLoop, calls=%fused_computation.197 | loop fusion | bytes 786432 | tf_op jit(solution)/shard_map/slice | solution.py:47
  3.9 2.5 %all_gather.18 = bf16[32,8,1024]{2,0,1:T(8,128)(2,1)S(1)} all-gather(bf16[32,4,1024]{2,0,1:T(8,128)(2,1)S(1)} %copy.168), channel_id=1, replica_groups=mesh['groups'=2,'rows'=4,'section'=2,'feat'=2] {'feat'}, dimensions={1}, use_global_device_ids=true | all-gather | bytes 786432 | tf_op jit(solution)/shard_map/all_gather | solution.py:54
  8.1 1.6 %fusion.115 = (f32[32,8,4]{2,1,0:T(8,128)S(1)}, f32[32,8,4,8]{3,2,1,0:T(4,128)}) fusion(bf16[32,8,8,64]{3,2,0,1:T(8,128)(2,1)S(1)} %reshape.275, bf16[32,4,8,64]{3,2,1,0:T(8,128)(2,1)S(1)} %reshape.284, pred[4,8]{1,0:T(4,128)(4,1)S(1)} %fusion.106), kind=kOutput, calls=%fused_computation.200 | convolution fusion | flops 1081351 | bytes 430112 | tf_op jit(solution)/shard_map/sub | solution.py:62
  9.6 1.7 %fusion.28 = bf16[32,4,8,64]{3,1,2,0:T(4,128)(2,1)S(1)} fusion(bf16[32,8,8,64]{3,2,0,1:T(8,128)(2,1)S(1)} %copy-done.11, f32[32,8,4,8]{3,2,1,0:T(4,128)} %get-tuple-element.27, f32[32,8,4]{2,1,0:T(8,128)S(1)} %get-tuple-element.26), kind=kOutput, calls=%fused_computation.44 | convolution fusion | flops 1130496 | bytes 430080 | tf_op jit(solution)/shard_map/rhij,rjhd->rihd/dot_general | solution.py:63
  12.8 10.9 %all-gather = bf16[1,2,16,4,512]{4,3,2,1,0:T(4,128)(2,1)S(1)} all-gather(bf16[1,2,4,4,512]{4,3,2,1,0:T(4,128)(2,1)S(1)} %copy-done.17), channel_id=2, replica_groups=mesh['groups'=2,'rows'=4,'section'=2,'feat'=2] {'rows'}, dimensions={2}, use_global_device_ids=true | all-gather | bytes 163840 | tf_op jit(solution)/shard_map/all_gather | solution.py:74
  24.8 1.7 %reshape.283 = bf16[16,4,8,64]{3,2,1,0:T(8,128)(2,1)} reshape(bf16[1,1,16,4,512]{4,3,2,1,0:T(4,128)(2,1)} %get-tuple-element.22) | data formatting | bytes 131072 | tf_op jit(solution)/shard_map/reshape | solution.py:78
  26.6 1.7 %fusion.27 = bf16[32,4,8,64]{3,0,2,1:T(8,128)(2,1)S(1)} fusion(f32[32,4,8]{0,2,1:T(8,128)S(1)} %fusion.87, f32[32,4,8,16]{0,3,2,1:T(8,128)} %copy-done.9, f32[32,4,8]{0,2,1:T(8,128)S(1)} %broadcast_maximum_fusion.3, bf16[16,4,8,64]{3,2,1,0:T(8,128)(2,1)} %reshape.283), kind=kOutput, calls=%fused_computation.43 | convolution fusion | flops 12730368 | bytes 270336 | tf_op jit(solution)/shard_map/rghn,nghd->rghd/dot_general | solution.py:86
  29.1 1.8 %dot_general.120 = bf16[32,4,512]{2,0,1:T(8,128)(2,1)} reshape(bf16[32,4,8,64]{3,2,0,1:T(8,128)(2,1)} %copy.95) | data formatting | bytes 262144 | tf_op jit(solution)/shard_map/dot_general | solution.py:90
  31.0 1.8 %fusion.36 = bf16[32,4,512]{2,0,1:T(8,128)(2,1)} fusion(f32[32,4,512]{2,0,1:T(8,128)S(1)} %get-tuple-element.29, bf16[32,4,512]{2,0,1:T(8,128)(2,1)} %dot_general.120, bf16[1,512,512]{2,1,0:T(8,128)(2,1)S(1)} %copy-done.3), kind=kOutput, calls=%fused_computation.64 | convolution fusion | flops 67239936 | bytes 1048576 | tf_op jit(solution)/shard_map/dot_general | solution.py:90
  32.8 1.3 collective-permute-start
  35.7 1.6 %constant_dynamic-slice_fusion.2 = bf16[1,32,4,512]{3,2,1,0:T(4,128)(2,1)} fusion(bf16[3,32,4,512]{3,2,1,0:T(4,128)(2,1)} %copy_dynamic-update-slice_fusion.3, s32[]{:T(128)S(6)} %min.14), kind=kLoop, calls=%fused_computation.190 | loop fusion | bytes 262148 | tf_op jit(solution)/shard_map/jit(dynamic_index_in_dim)/dynamic_slice | solution.py:95
  37.3 1.4 collective-permute-done
  41.7 1.8 %reshape.246 = bf16[32,4,1536]{2,1,0:T(4,128)(2,1)} reshape(bf16[128,1536]{1,0:T(8,128)(2,1)} %convolution_convert_fusion.2) | data formatting | bytes 786432 | tf_op jit(solution)/shard_map/reshape | solution.py:52
  44.7 6.2 %all_gather.20 = bf16[32,8,1024]{2,0,1:T(8,128)(2,1)S(1)} all-gather(bf16[32,4,1024]{2,0,1:T(8,128)(2,1)S(1)} %copy.171), channel_id=1, replica_groups=mesh['groups'=2,'rows'=4,'section'=2,'feat'=2] {'feat'}, dimensions={1}, use_global_device_ids=true | all-gather | bytes 786432 | tf_op jit(solution)/shard_map/all_gather | solution.py:54
  51.8 2.1 %reshape.277 = bf16[32,8,8,64]{3,2,0,1:T(8,128)(2,1)} reshape(bf16[32,8,512]{2,0,1:T(8,128)(2,1)} %get-tuple-element.15) | data formatting | bytes 524288 | tf_op jit(solution)/shard_map/reshape | solution.py:56
  54.7 2.1 %reshape.276 = bf16[32,8,8,64]{3,2,0,1:T(8,128)(2,1)} reshape(bf16[32,8,512]{2,0,1:T(8,128)(2,1)} %get-tuple-element.16) | data formatting | bytes 524288 | tf_op jit(solution)/shard_map/reshape | solution.py:57
  56.8 2.7 %fusion.117 = (f32[32,8,4]{2,1,0:T(8,128)S(1)}, f32[32,8,4,8]{3,2,1,0:T(4,128)}) fusion(bf16[32,8,8,64]{3,2,0,1:T(8,128)(2,1)} %reshape.277, bf16[32,4,8,64]{3,2,1,0:T(8,128)(2,1)} %reshape.285, pred[4,8]{1,0:T(4,128)(4,1)S(1)} %copy-done.20), kind=kOutput, calls=%fused_computation.202 | convolution fusion | flops 1081351 | bytes 430112 | tf_op jit(solution)/shard_map/sub | solution.py:62
  59.5 1.8 %fusion.29 = bf16[32,4,8,64]{3,1,2,0:T(4,128)(2,1)S(1)} fusion(bf16[32,8,8,64]{3,2,0,1:T(8,128)(2,1)} %reshape.276, f32[32,8,4,8]{3,2,1,0:T(4,128)} %get-tuple-element.33, f32[32,8,4]{2,1,0:T(8,128)S(1)} %get-tuple-element.32), kind=kOutput, calls=%fused_computation.45 | convolution fusion | flops 1130496 | bytes 430080 | tf_op jit(solution)/shard_map/rhij,rjhd->rihd/dot_general | solution.py:63
  62.2 1.3 multiply_reduce_fusion.2
  64.4 1.6 %reshape.250 = bf16[128,512]{1,0:T(8,128)(2,1)} reshape(bf16[32,4,512]{2,1,0:T(4,128)(2,1)} %copy.107) | data formatting | bytes 262144 | tf_op jit(solution)/shard_map/reshape | solution.py:70
  66.0 1.8 %convolution_convert_fusion.10 = bf16[128,512]{1,0:T(8,128)(2,1)} fusion(bf16[128,512]{1,0:T(8,128)(2,1)} %reshape.250, bf16[1,512,512]{2,1,0:T(8,128)(2,1)S(1)} %copy-done.1), kind=kOutput, calls=%fused_computation.70 | convolution fusion | flops 67174400 | bytes 786432 | tf_op jit(solution)/shard_map/dot_general | solution.py:71
  67.8 1.8 %reshape.251 = bf16[32,4,8,64]{3,2,1,0:T(8,128)(2,1)} reshape(bf16[128,512]{1,0:T(8,128)(2,1)} %convolution_convert_fusion.10) | data formatting | bytes 262144 | tf_op jit(solution)/shard_map/reshape | solution.py:72
  70.9 1.6 %fusion.26 = bf16[32,4,8,64]{3,0,2,1:T(8,128)(2,1)S(1)} fusion(f32[32,4,8]{0,2,1:T(8,128)S(1)} %fusion.88, f32[32,4,8,16]{0,3,2,1:T(8,128)S(1)} %get-tuple-element.37, f32[32,4,8]{0,2,1:T(8,128)S(1)} %broadcast_maximum_fusion.2, bf16[16,4,8,64]{3,2,1,0:T(8,128)(2,1)} %reshape.283), kind=kOutput, calls=%fused_computation.42 | convolution fusion | flops 12730368 | bytes 270336 | tf_op jit(solution)/shard_map/rghn,nghd->rghd/dot_general | solution.py:86
  73.2 1.8 %dot_general.130 = bf16[32,4,512]{2,0,1:T(8,128)(2,1)} reshape(bf16[32,4,8,64]{3,2,0,1:T(8,128)(2,1)} %copy.111) | data formatting | bytes 262144 | tf_op jit(solution)/shard_map/dot_general | solution.py:90
  76.2 1.3 collective-permute-start.1
  79.2 1.6 %constant_dynamic-slice_fusion.1 = bf16[1,32,4,512]{3,2,1,0:T(4,128)(2,1)} fusion(bf16[3,32,4,512]{3,2,1,0:T(4,128)(2,1)} %copy_dynamic-update-slice_fusion.2, s32[]{:T(128)S(6)} %min.15), kind=kLoop, calls=%fused_computation.189 | loop fusion | bytes 262148 | tf_op jit(solution)/shard_map/jit(dynamic_index_in_dim)/dynamic_slice | solution.py:95
  80.8 2.0 %collective-permute-done.1 = bf16[32,4,512]{2,0,1:T(8,128)(2,1)S(1)} collective-permute-done((bf16[32,4,512]{2,0,1:T(8,128)(2,1)S(1)}, bf16[32,4,512]{2,0,1:T(8,128)(2,1)S(1)}, u32[]{:S(2)}, u32[]{:S(2)}) %collective-permute-start.1) | collective-permute-done | bytes 131104 | tf_op jit(solution)/shard_map/ppermute | solution.py:15
  85.0 1.8 %reshape.253 = bf16[32,4,1536]{2,1,0:T(4,128)(2,1)} reshape(bf16[128,1536]{1,0:T(8,128)(2,1)} %convolution_convert_fusion.1) | data formatting | bytes 786432 | tf_op jit(solution)/shard_map/reshape | solution.py:52
  88.0 3.0 %all_gather.21 = bf16[32,8,1024]{2,0,1:T(8,128)(2,1)S(1)} all-gather(bf16[32,4,1024]{2,0,1:T(8,128)(2,1)S(1)} %copy.174), channel_id=1, replica_groups=mesh['groups'=2,'rows'=4,'section'=2,'feat'=2] {'feat'}, dimensions={1}, use_global_device_ids=true | all-gather | bytes 786432 | tf_op jit(solution)/shard_map/all_gather | solution.py:54
  91.9 2.1 %reshape.279 = bf16[32,8,8,64]{3,2,0,1:T(8,128)(2,1)} reshape(bf16[32,8,512]{2,0,1:T(8,128)(2,1)} %get-tuple-element.13) | data formatting | bytes 524288 | tf_op jit(solution)/shard_map/reshape | solution.py:56
  94.8 2.1 %reshape.278 = bf16[32,8,8,64]{3,2,0,1:T(8,128)(2,1)} reshape(bf16[32,8,512]{2,0,1:T(8,128)(2,1)} %get-tuple-element.14) | data formatting | bytes 524288 | tf_op jit(solution)/shard_map/reshape | solution.py:57
  96.9 2.7 %fusion.119 = (f32[32,8,4]{2,1,0:T(8,128)S(1)}, f32[32,8,4,8]{3,2,1,0:T(4,128)}) fusion(bf16[32,8,8,64]{3,2,0,1:T(8,128)(2,1)} %reshape.279, bf16[32,4,8,64]{3,2,1,0:T(8,128)(2,1)} %reshape.286, pred[4,8]{1,0:T(4,128)(4,1)S(1)} %copy-done.20), kind=kOutput, calls=%fused_computation.204 | convolution fusion | flops 1081351 | bytes 430112 | tf_op jit(solution)/shard_map/sub | solution.py:62
  99.6 1.8 %fusion.30 = bf16[32,4,8,64]{3,1,2,0:T(4,128)(2,1)S(1)} fusion(bf16[32,8,8,64]{3,2,0,1:T(8,128)(2,1)} %reshape.278, f32[32,8,4,8]{3,2,1,0:T(4,128)} %get-tuple-element.39, f32[32,8,4]{2,1,0:T(8,128)S(1)} %get-tuple-element.38), kind=kOutput, calls=%fused_computation.46 | convolution fusion | flops 1130496 | bytes 430080 | tf_op jit(solution)/shard_map/rhij,rjhd->rihd/dot_general | solution.py:63
  102.3 1.3 multiply_reduce_fusion.1
  104.5 1.6 %reshape.257 = bf16[128,512]{1,0:T(8,128)(2,1)} reshape(bf16[32,4,512]{2,1,0:T(4,128)(2,1)} %copy.124) | data formatting | bytes 262144 | tf_op jit(solution)/shard_map/reshape | solution.py:70
  106.0 1.8 %convolution_convert_fusion.9 = bf16[128,512]{1,0:T(8,128)(2,1)} fusion(bf16[128,512]{1,0:T(8,128)(2,1)} %reshape.257, bf16[1,512,512]{2,1,0:T(8,128)(2,1)S(1)} %copy-done.1), kind=kOutput, calls=%fused_computation.69 | convolution fusion | flops 67174400 | bytes 786432 | tf_op jit(solution)/shard_map/dot_general | solution.py:71
  107.8 1.8 %reshape.258 = bf16[32,4,8,64]{3,2,1,0:T(8,128)(2,1)} reshape(bf16[128,512]{1,0:T(8,128)(2,1)} %convolution_convert_fusion.9) | data formatting | bytes 262144 | tf_op jit(solution)/shard_map/reshape | solution.py:72
  110.9 1.6 %fusion.25 = bf16[32,4,8,64]{3,0,2,1:T(8,128)(2,1)S(1)} fusion(f32[32,4,8]{0,2,1:T(8,128)S(1)} %fusion.89, f32[32,4,8,16]{0,3,2,1:T(8,128)S(1)} %get-tuple-element.43, f32[32,4,8]{0,2,1:T(8,128)S(1)} %broadcast_maximum_fusion.1, bf16[16,4,8,64]{3,2,1,0:T(8,128)(2,1)} %reshape.283), kind=kOutput, calls=%fused_computation.41 | convolution fusion | flops 12730368 | bytes 270336 | tf_op jit(solution)/shard_map/rghn,nghd->rghd/dot_general | solution.py:86
  113.3 1.8 %dot_general.140 = bf16[32,4,512]{2,0,1:T(8,128)(2,1)} reshape(bf16[32,4,8,64]{3,2,0,1:T(8,128)(2,1)} %copy.128) | data formatting | bytes 262144 | tf_op jit(solution)/shard_map/dot_general | solution.py:90
  116.3 1.3 collective-permute-start.2
  119.3 1.6 %constant_dynamic-slice_fusion = bf16[1,32,4,512]{3,2,1,0:T(4,128)(2,1)} fusion(bf16[3,32,4,512]{3,2,1,0:T(4,128)(2,1)} %copy_dynamic-update-slice_fusion.1, s32[]{:T(128)S(6)} %min.16), kind=kLoop, calls=%fused_computation.188 | loop fusion | bytes 262148 | tf_op jit(solution)/shard_map/jit(dynamic_index_in_dim)/dynamic_slice | solution.py:95
  120.9 2.0 %collective-permute-done.2 = bf16[32,4,512]{2,0,1:T(8,128)(2,1)S(1)} collective-permute-done((bf16[32,4,512]{2,0,1:T(8,128)(2,1)S(1)}, bf16[32,4,512]{2,0,1:T(8,128)(2,1)S(1)}, u32[]{:S(2)}, u32[]{:S(2)}) %collective-permute-start.2) | collective-permute-done | bytes 131104 | tf_op jit(solution)/shard_map/ppermute | solution.py:15
  125.1 1.8 %reshape.260 = bf16[32,4,1536]{2,1,0:T(4,128)(2,1)} reshape(bf16[128,1536]{1,0:T(8,128)(2,1)} %convolution_convert_fusion) | data formatting | bytes 786432 | tf_op jit(solution)/shard_map/reshape | solution.py:52
  128.1 3.2 %all_gather.22 = bf16[32,8,1024]{2,0,1:T(8,128)(2,1)S(1)} all-gather(bf16[32,4,1024]{2,0,1:T(8,128)(2,1)S(1)} %copy.176), channel_id=1, replica_groups=mesh['groups'=2,'rows'=4,'section'=2,'feat'=2] {'feat'}, dimensions={1}, use_global_device_ids=true | all-gather | bytes 786432 | tf_op jit(solution)/shard_map/all_gather | solution.py:54
  132.2 2.1 %reshape.281 = bf16[32,8,8,64]{3,2,0,1:T(8,128)(2,1)} reshape(bf16[32,8,512]{2,0,1:T(8,128)(2,1)} %get-tuple-element.11) | data formatting | bytes 524288 | tf_op jit(solution)/shard_map/reshape | solution.py:56
  135.1 2.1 %reshape.280 = bf16[32,8,8,64]{3,2,0,1:T(8,128)(2,1)} reshape(bf16[32,8,512]{2,0,1:T(8,128)(2,1)} %get-tuple-element.12) | data formatting | bytes 524288 | tf_op jit(solution)/shard_map/reshape | solution.py:57
  137.2 2.7 %fusion.121 = (f32[32,8,4]{2,1,0:T(8,128)S(1)}, f32[32,8,4,8]{3,2,1,0:T(4,128)}) fusion(bf16[32,8,8,64]{3,2,0,1:T(8,128)(2,1)} %reshape.281, bf16[32,4,8,64]{3,2,1,0:T(8,128)(2,1)} %reshape.287, pred[4,8]{1,0:T(4,128)(4,1)S(1)} %copy-done.20), kind=kOutput, calls=%fused_computation.206 | convolution fusion | flops 1081351 | bytes 430112 | tf_op jit(solution)/shard_map/sub | solution.py:62
  139.9 1.8 %fusion.31 = bf16[32,4,8,64]{3,1,2,0:T(4,128)(2,1)S(1)} fusion(bf16[32,8,8,64]{3,2,0,1:T(8,128)(2,1)} %reshape.280, f32[32,8,4,8]{3,2,1,0:T(4,128)} %get-tuple-element.45, f32[32,8,4]{2,1,0:T(8,128)S(1)} %get-tuple-element.44), kind=kOutput, calls=%fused_computation.47 | convolution fusion | flops 1130496 | bytes 430080 | tf_op jit(solution)/shard_map/rhij,rjhd->rihd/dot_general | solution.py:63
  (154 shorter events, 43.0 us)
Async XLA Ops:
  0.0 3.1 %copy-start = (bf16[1,512,1536]{2,1,0:T(8,128)(2,1)S(1)}, bf16[1,512,1536]{2,1,0:T(8,128)(2,1)}, u32[]{:S(2)}) copy-start(bf16[1,512,1536]{2,1,0:T(8,128)(2,1)} %param.11) | copy-start | bytes 4718596
  2.9 0.8 copy-start.15
  2.9 9.1 %copy-start.13 = (f32[1,1,512]{2,1,0:T(1,128)}, f32[1,1,512]{2,1,0:T(1,128)S(1)}, u32[]{:S(2)}) copy-start(f32[1,1,512]{2,1,0:T(1,128)S(1)} %get-tuple-element.24) | copy-start | bytes 6148
  6.4 1.6 %copy-start.18 = (s32[8,8]{1,0:T(8,128)S(1)}, s32[8,8]{1,0:T(8,128)}, u32[]{:S(2)}) copy-start(s32[8,8]{1,0:T(8,128)} %param.10) | copy-start | bytes 772
  8.0 1.6 %copy-start.11 = (bf16[32,8,8,64]{3,2,0,1:T(8,128)(2,1)S(1)}, bf16[32,8,8,64]{3,2,0,1:T(8,128)(2,1)}, u32[]{:S(2)}) copy-start(bf16[32,8,8,64]{3,2,0,1:T(8,128)(2,1)} %reshape.274) | copy-start | bytes 786436
  8.1 1.6 %copy-start.19 = (pred[4,8]{1,0:T(4,128)(4,1)}, pred[4,8]{1,0:T(4,128)(4,1)S(1)}, u32[]{:S(2)}) copy-start(pred[4,8]{1,0:T(4,128)(4,1)S(1)} %fusion.106) | copy-start | bytes 100
  9.6 2.0 %copy-start.2 = (bf16[1,512,512]{2,1,0:T(8,128)(2,1)S(1)}, bf16[1,512,512]{2,1,0:T(8,128)(2,1)}, u32[]{:S(2)}) copy-start(bf16[1,512,512]{2,1,0:T(8,128)(2,1)} %param.12) | copy-start | bytes 1572868
  11.3 1.0 copy-start.1
  11.6 1.2 copy-start.17
  24.8 1.7 %copy-start.9 = (f32[32,4,8,16]{0,3,2,1:T(8,128)}, f32[32,4,8,16]{0,3,2,1:T(8,128)S(1)}, u32[]{:S(2)}) copy-start(f32[32,4,8,16]{0,3,2,1:T(8,128)S(1)} %get-tuple-element.31) | copy-start | bytes 196612
  26.6 4.3 %copy-start.3 = (bf16[1,512,512]{2,1,0:T(8,128)(2,1)S(1)}, bf16[1,512,512]{2,1,0:T(8,128)(2,1)}, u32[]{:S(2)}) copy-start(bf16[1,512,512]{2,1,0:T(8,128)(2,1)} %param.14) | copy-start | bytes 1572868
  29.1 11.2 %copy-start.16 = (f32[1,1,512]{2,1,0:T(1,128)S(1)}, f32[1,1,512]{2,1,0:T(1,128)}, u32[]{:S(2)}) copy-start(f32[1,1,512]{2,1,0:T(1,128)} %copy-done.15) | copy-start | bytes 6148
  32.8 5.9 %collective-permute-start = (bf16[32,4,512]{2,0,1:T(8,128)(2,1)}, bf16[32,4,512]{2,0,1:T(8,128)(2,1)S(1)}, u32[]{:S(2)}, u32[]{:S(2)}) collective-permute-start(bf16[32,4,512]{2,0,1:T(8,128)(2,1)} %fusion.36), channel_id=1, source_target_pairs={{0,2},{1,3},{4,6},{5,7},{8,10},{9,11},{12,14},{13,15},{16,18},{17,... | collective-permute-start | bytes 393224 | tf_op jit(solution)/shard_map/ppermute | solution.py:15
  39.7 0.7 copy-start.7
  44.6 9.2 %slice-start = ((bf16[32,4,1536]{2,1,0:T(4,128)(2,1)}), bf16[32,4,512]{2,1,0:T(4,128)(2,1)S(1)}, s32[]{:S(2)}) async-start(bf16[32,4,1536]{2,1,0:T(4,128)(2,1)} %reshape.246), calls=%async_computation | async-start | bytes 262144 | tf_op jit(solution)/shard_map/slice | solution.py:53
  50.9 5.9 %copy-start.20 = (pred[4,8]{1,0:T(4,128)(4,1)S(1)}, pred[4,8]{1,0:T(4,128)(4,1)}, u32[]{:S(2)}) copy-start(pred[4,8]{1,0:T(4,128)(4,1)} %copy-done.19) | copy-start | bytes 100
  61.3 2.2 %copy-start.14 = (f32[1,1,512]{2,1,0:T(1,128)S(1)}, f32[1,1,512]{2,1,0:T(1,128)}, u32[]{:S(2)}) copy-start(f32[1,1,512]{2,1,0:T(1,128)} %copy-done.13) | copy-start | bytes 6148
  75.1 7.8 %copy-start.4 = (bf16[1,32,4,512]{3,2,1,0:T(4,128)(2,1)S(1)}, bf16[1,32,4,512]{3,2,1,0:T(4,128)(2,1)}, u32[]{:S(2)}) copy-start(bf16[1,32,4,512]{3,2,1,0:T(4,128)(2,1)} %get-tuple-element.19) | copy-start | bytes 393220
  76.2 6.6 %collective-permute-start.1 = (bf16[32,4,512]{2,0,1:T(8,128)(2,1)S(1)}, bf16[32,4,512]{2,0,1:T(8,128)(2,1)S(1)}, u32[]{:S(2)}, u32[]{:S(2)}) collective-permute-start(bf16[32,4,512]{2,0,1:T(8,128)(2,1)S(1)} %fusion.37), channel_id=1, source_target_pairs={{0,2},{1,3},{4,6},{5,7},{8,10},{9,11},{12,14},{13,15},{16,18},{17,... | collective-permute-start | bytes 393224 | tf_op jit(solution)/shard_map/ppermute | solution.py:15
  83.0 0.7 copy-start.8
  87.9 6.0 %slice-start.1 = ((bf16[32,4,1536]{2,1,0:T(4,128)(2,1)}), bf16[32,4,512]{2,1,0:T(4,128)(2,1)S(1)}, s32[]{:S(2)}) async-start(bf16[32,4,1536]{2,1,0:T(4,128)(2,1)} %reshape.253), calls=%async_computation.1 | async-start | bytes 262144 | tf_op jit(solution)/shard_map/slice | solution.py:53
  115.1 7.8 %copy-start.5 = (bf16[1,32,4,512]{3,2,1,0:T(4,128)(2,1)S(1)}, bf16[1,32,4,512]{3,2,1,0:T(4,128)(2,1)}, u32[]{:S(2)}) copy-start(bf16[1,32,4,512]{3,2,1,0:T(4,128)(2,1)} %get-tuple-element.19) | copy-start | bytes 393220
  116.3 6.6 %collective-permute-start.2 = (bf16[32,4,512]{2,0,1:T(8,128)(2,1)S(1)}, bf16[32,4,512]{2,0,1:T(8,128)(2,1)S(1)}, u32[]{:S(2)}, u32[]{:S(2)}) collective-permute-start(bf16[32,4,512]{2,0,1:T(8,128)(2,1)S(1)} %fusion.38), channel_id=1, source_target_pairs={{0,2},{1,3},{4,6},{5,7},{8,10},{9,11},{12,14},{13,15},{16,18},{17,... | collective-permute-start | bytes 393224 | tf_op jit(solution)/shard_map/ppermute | solution.py:15
  123.1 0.7 copy-start.6
  128.0 6.2 %slice-start.2 = ((bf16[32,4,1536]{2,1,0:T(4,128)(2,1)}), bf16[32,4,512]{2,1,0:T(4,128)(2,1)S(1)}, s32[]{:S(2)}) async-start(bf16[32,4,1536]{2,1,0:T(4,128)(2,1)} %reshape.260), calls=%async_computation.2 | async-start | bytes 262144 | tf_op jit(solution)/shard_map/slice | solution.py:53
  143.9 1.1 copy-start.12
  145.0 1.0 copy-start.10
where the time goes:
time: 149 us; the launch traced here: 147 us
  local copies, waits for them, and re-layouts  65.1 us (44%)
  matrix products  41.6 us (28%)
  blocking collectives  25.8 us (17%)
  waiting for transfers between devices  5.37 us (4%)
  other arithmetic  4.52 us (3%)
  starting transfers between devices  3.86 us (3%)
    all_gather x4, blocking collectives, per_device(): pairs = lax.all_gather(qkv[:, :, width:], 'feat', axis=1, tiled=True)  14.9 us
    all_gather x1, blocking collectives, per_device(): piece = lax.all_gather(cache, 'rows', axis=1, tiled=True)  10.9 us
    sub x4, matrix products, per_device(): weights = jax.nn.softmax(scores, axis=-1).astype(jnp.bfloat16)  9.65 us
    reshape x4, local copies, waits for them, and re-layouts, per_device(): values = pairs[:, :, width:].reshape(test_n, groups, heads, head_dim)  7.3 us
    dot_general x4, matrix products, per_device(): jnp.einsum('rhij,rjhd->rihd', weights, values, preferred_element_type=jnp...  7.15 us
    reshape x4, local copies, waits for them, and re-layouts, per_device(): keys = pairs[:, :, :width].reshape(test_n, groups, heads, head_dim)  6.44 us
    dot_general x4, local copies, waits for them, and re-layouts, per_device(): term = jnp.dot(item_mix, witem, preferred_element_type=jnp.float32)  5.67 us
    reshape x4, local copies, waits for them, and re-layouts, per_device(): qkv = qkv.reshape(test_n, group_dev, 3 * width)  5.63 us
  transfers between devices with their start and end apart: 3, of which 3 were waited for; matrix products, arithmetic and copies ran while one was open for 7% of the time, Pallas kernels for 0%

commit v1 on v0

v1 whole, which is shorter than its diff:
```python
import functools
import math

import jax
import jax.numpy as jnp
from jax import lax
from jax.experimental import pallas as pl
from jax.experimental.pallas import tpu as pltpu
from jax.sharding import PartitionSpec as P

HEADS = 8
MESH = pl.DeviceIdType.MESH
F32 = jnp.float32
BF16 = jnp.bfloat16
EXCLUDED = -1e30


def iota(shape, dim):
    return lax.broadcasted_iota(jnp.int32, shape, dim)


def normed(x, gain):
    mean_sq = jnp.mean(x * x, axis=-1, keepdims=True)
    return (x * lax.rsqrt(mean_sq + 1e-06) * gain).astype(BF16)


def dot(a, b):
    return jnp.dot(a, b, preferred_element_type=F32)


def dot_t(a, b):
    return lax.dot_general(a, b, (((1,), (1,)), ((), ())), preferred_element_type=F32)


def kernel(
    sizes, rows_hbm, cache_hbm, pattern_ref, qkv_hbm, out_hbm, query_hbm, item_hbm, gains_ref, hidden_hbm,
    x_in, wqkv, wout, wquery, witem, h_buf, h_out, q_buf, kv_buf, cache_buf, k_stack, v_stack, feat_bias, item_bias, staged,
    weight_sem, x_sem, own_sem, out_sem, kv_send, kv_recv, cache_send, cache_recv, h_send, h_recv,
):
    sections, row_devs = sizes
    micro, test_n, gd, width = x_in.shape
    tokens = test_n * gd
    pair_w = 2 * (width // HEADS)
    pairs = width // pair_w
    half = tokens // 2
    half_rows = test_n // 2
    train_dev = cache_buf.shape[2]
    nk = row_devs * train_dev * gd
    factor = math.log2(math.e) / math.sqrt(width // HEADS)

    section = lax.axis_index("section")
    row = lax.axis_index("rows")
    feat = lax.axis_index("feat")
    partner = 1 - feat
    first = section == 0
    receives = section > 0
    sends = section < sections - 1

    weights = [
        pltpu.make_async_copy(src.at[0], dst, weight_sem.at[i])
        for i, (src, dst) in enumerate(
            [(qkv_hbm, wqkv), (out_hbm, wout), (query_hbm, wquery), (item_hbm, witem)]
        )
    ]

    def x_copy(m):
        return pltpu.make_async_copy(rows_hbm.at[m], x_in.at[m], x_sem.at[m])

    @pl.when(first)
    def _():
        for m in range(micro):
            x_copy(m).start()

    for copy in weights:
        copy.start()
    own_cache = pltpu.make_async_copy(cache_hbm.at[0], cache_buf.at[row], own_sem)
    own_cache.start()

    barrier = pltpu.get_barrier_semaphore()
    pl.semaphore_signal(barrier, inc=1, device_id={"feat": partner}, device_id_type=MESH)
    for off in range(1, row_devs):
        pl.semaphore_signal(
            barrier, inc=1, device_id={"rows": lax.rem(row + off, row_devs)}, device_id_type=MESH
        )

    @pl.when(receives)
    def _():
        pl.semaphore_signal(barrier, inc=1, device_id={"section": section - 1}, device_id_type=MESH)

    @pl.when(sends)
    def _():
        pl.semaphore_signal(barrier, inc=1, device_id={"section": section + 1}, device_id_type=MESH)

    pl.semaphore_wait(
        barrier, row_devs + jnp.where(receives, 1, 0) + jnp.where(sends, 1, 0)
    )

    def cache_copy(off):
        return pltpu.make_async_remote_copy(
            src_ref=cache_hbm.at[0], dst_ref=cache_buf.at[row],
            send_sem=cache_send.at[off - 1], recv_sem=cache_recv.at[row],
            device_id={"rows": lax.rem(row + off, row_devs)}, device_id_type=MESH,
        )

    def cache_arrival(off):
        source = lax.rem(row + off, row_devs)
        return pltpu.make_async_remote_copy(
            src_ref=cache_hbm.at[0], dst_ref=cache_buf.at[source],
            send_sem=cache_send.at[off - 1], recv_sem=cache_recv.at[source],
            device_id={"rows": source}, device_id_type=MESH,
        )

    for off in range(1, row_devs):
        cache_copy(off).start()

    def kv_copy(m):
        return pltpu.make_async_remote_copy(
            src_ref=kv_buf.at[m, 0], dst_ref=kv_buf.at[m, 1],
            send_sem=kv_send.at[m], recv_sem=kv_recv.at[m],
            device_id={"feat": partner}, device_id_type=MESH,
        )

    def h_copy(m, target):
        return pltpu.make_async_remote_copy(
            src_ref=h_out.at[m], dst_ref=h_buf.at[m],
            send_sem=h_send.at[m], recv_sem=h_recv.at[m],
            device_id={"section": target}, device_id_type=MESH,
        )

    def out_copy(m):
        return pltpu.make_async_copy(staged.at[m], hidden_hbm.at[0, m], out_sem.at[m])

    groups = 2 * gd
    q_at = iota((half, groups), 0) % gd + feat * gd
    pick_q = (q_at == iota((half, groups), 1)).astype(F32)
    key = iota((groups, 2 * half), 1)
    k_at = key % gd + jnp.where(key < half, feat, partner) * gd
    pick_k = (k_at == iota((groups, 2 * half), 0)).astype(F32)
    pattern = (pattern_ref[...] != 0).astype(F32)
    seen = dot(dot(pick_q, pattern), pick_k) > 0.5
    qi, ki = iota((half, 2 * half), 0), iota((half, 2 * half), 1)
    seen = seen | (qi == ki)
    seen = seen & (qi // gd == (ki % half) // gd)
    bias = jnp.where(seen, 0.0, EXCLUDED).astype(F32)
    feat_bias[...] = jnp.concatenate([bias, bias], axis=0)
    item_bias[...] = jnp.where(
        iota((tokens, 2 * nk), 0) % gd == iota((tokens, 2 * nk), 1) % gd, 0.0, EXCLUDED
    ).astype(F32)

    def project(m):
        @pl.when(first)
        def _():
            x_copy(m).wait()
            h_buf[m] = x_in[m].astype(F32).reshape(tokens, width).astype(BF16)

        @pl.when(receives)
        def _():
            h_copy(m, section - 1).wait_recv()

        a = normed(h_buf[m].astype(F32), gains_ref[0, 0:1, :])
        kv_buf[m, 0, :, :width] = dot(a, wqkv[:, width : 2 * width]).astype(BF16)
        kv_buf[m, 0, :, width:] = dot(a, wqkv[:, 2 * width :]).astype(BF16)
        kv_copy(m).start()
        q_buf[m] = dot(a, wqkv[:, :width]).astype(BF16)

    low_half = iota((half, pair_w), 1) < pair_w // 2
    ones = jnp.ones((2 * half, pair_w), BF16)

    def feature_mix(m):
        blocks = []
        for block in range(2):
            span = pl.ds(block * half, half)
            mixed = []
            for pair in range(pairs):
                lanes = slice(pair * pair_w, (pair + 1) * pair_w)
                v_lanes = slice(width + pair * pair_w, width + (pair + 1) * pair_w)
                q = q_buf[m, span, lanes]
                zero = jnp.zeros_like(q)
                q2 = jnp.concatenate([jnp.where(low_half, q, zero), jnp.where(low_half, zero, q)], axis=0)
                k = jnp.concatenate([kv_buf[m, 0, span, lanes], kv_buf[m, 1, span, lanes]], axis=0)
                v = jnp.concatenate([kv_buf[m, 0, span, v_lanes], kv_buf[m, 1, span, v_lanes]], axis=0)
                s = dot_t(q2, k) * factor + feat_bias[...]
                p = jnp.exp2(s - jnp.max(s, axis=-1, keepdims=True)).astype(BF16)
                o = dot(p, jnp.concatenate([v, ones], axis=1))
                o = o[:, :pair_w] / o[:, pair_w:]
                mixed.append(jnp.where(low_half, o[:half], o[half:]))
            blocks.append(jnp.concatenate(mixed, axis=1))
        return jnp.concatenate(blocks, axis=0).astype(BF16)

    low_keys = iota((tokens, 2 * nk), 1) < nk

    def item_mix(query):
        mixed = []
        for pair in range(pairs):
            lanes = slice(pair * pair_w, (pair + 1) * pair_w)
            s = dot_t(query[:, lanes], k_stack[pair]) * factor + item_bias[...]
            low = jnp.max(jnp.where(low_keys, s, -jnp.inf), axis=-1, keepdims=True)
            high = jnp.max(jnp.where(low_keys, -jnp.inf, s), axis=-1, keepdims=True)
            p = jnp.exp2(s - jnp.where(low_keys, low, high)).astype(BF16)
            o = dot(p, v_stack[pair])
            mixed.append(o[:, :pair_w] / o[:, pair_w:])
        return jnp.concatenate(mixed, axis=1).astype(BF16)

    weights[0].wait()
    project(0)

    def step(m, carry):
        @pl.when(m + 1 < micro)
        def _():
            project(m + 1)

        kv_copy(m).wait_recv()
        mixed = feature_mix(m)

        @pl.when(m == 0)
        def _():
            weights[1].wait()
            weights[2].wait()
            weights[3].wait()
            own_cache.wait()
            for off in range(1, row_devs):
                cache_arrival(off).wait_recv()
            side = iota((nk, pair_w), 1) < pair_w // 2
            one = jnp.where(side, 1.0, 0.0).astype(BF16)
            for pair in range(pairs):
                lanes = slice(pair * pair_w, (pair + 1) * pair_w)
                k = cache_buf[:, 0, :, :, lanes].astype(F32).reshape(nk, pair_w).astype(BF16)
                v = cache_buf[:, 1, :, :, lanes].astype(F32).reshape(nk, pair_w).astype(BF16)
                zero = jnp.zeros_like(k)
                k_stack[pair] = jnp.concatenate([jnp.where(side, k, zero), jnp.where(side, zero, k)], axis=0)
                v_stack[pair] = jnp.concatenate(
                    [
                        jnp.concatenate([jnp.where(side, v, zero), one], axis=1),
                        jnp.concatenate([jnp.where(side, zero, v), 1 - one], axis=1),
                    ],
                    axis=0,
                )

        h1 = h_buf[m].astype(F32) + dot(mixed, wout[...])
        b = normed(h1, gains_ref[0, 1:2, :])
        query = dot(b, wquery[...]).astype(BF16)
        result = h1 + dot(item_mix(query), witem[...])
        h_out[m] = result.astype(BF16)

        @pl.when(sends)
        def _():
            h_copy(m, section + 1).start()

        staged[m] = result.reshape(test_n, gd, width).astype(BF16)
        out_copy(m).start()
        return carry

    lax.fori_loop(0, micro, step, 0)

    for m in range(micro):
        kv_copy(m).wait_send()
        out_copy(m).wait()

    @pl.when(sends)
    def _():
        for m in range(micro):
            h_copy(m, section + 1).wait_send()

    for off in range(1, row_devs):
        cache_copy(off).wait_send()


def per_device(sizes, test_rows, train_cache, pattern, feat_qkv, feat_out, item_query, item_out, gains):
    sections, row_devs = sizes
    micro, test_n, gd, width = test_rows.shape
    train_dev = train_cache.shape[2]
    tokens = test_n * gd
    nk = row_devs * train_dev * gd
    pair_w = 2 * (width // HEADS)
    pairs = width // pair_w
    anywhere = pl.BlockSpec(memory_space=pl.ANY)
    vmem = pl.BlockSpec(memory_space=pltpu.VMEM)
    dma = pltpu.SemaphoreType.DMA
    return pl.pallas_call(
        functools.partial(kernel, sizes),
        out_shape=jax.ShapeDtypeStruct((1, micro, test_n, gd, width), BF16),
        in_specs=[anywhere, anywhere, vmem, anywhere, anywhere, anywhere, anywhere, vmem],
        out_specs=anywhere,
        scratch_shapes=[
            pltpu.VMEM((micro, test_n, gd, width), BF16),
            pltpu.VMEM((width, 3 * width), BF16),
            pltpu.VMEM((width, width), BF16),
            pltpu.VMEM((width, width), BF16),
            pltpu.VMEM((width, width), BF16),
            pltpu.VMEM((micro, tokens, width), BF16),
            pltpu.VMEM((micro, tokens, width), BF16),
            pltpu.VMEM((micro, tokens, width), BF16),
            pltpu.VMEM((micro, 2, tokens, 2 * width), BF16),
            pltpu.VMEM((row_devs, 2, train_dev, gd, width), BF16),
            pltpu.VMEM((pairs, 2 * nk, pair_w), BF16),
            pltpu.VMEM((pairs, 2 * nk, 2 * pair_w), BF16),
            pltpu.VMEM((tokens, tokens), F32),
            pltpu.VMEM((tokens, 2 * nk), F32),
            pltpu.VMEM((micro, test_n, gd, width), BF16),
            dma((4,)),
            dma((micro,)),
            dma(()),
            dma((micro,)),
            dma((micro,)),
            dma((micro,)),
            dma((row_devs - 1,)),
            dma((row_devs,)),
            dma((micro,)),
            dma((micro,)),
        ],
        compiler_params=pltpu.CompilerParams(
            collective_id=0, has_side_effects=True, vmem_limit_bytes=60 * 1024 * 1024
        ),
    )(test_rows, train_cache, pattern, feat_qkv, feat_out, item_query, item_out, gains)


def solution(mesh):
    sizes = (mesh.shape["section"], mesh.shape["rows"])
    return jax.shard_map(
        functools.partial(per_device, sizes),
        mesh=mesh,
        in_specs=(
            P(None, ("groups", "rows"), "feat", None),
            P("section", None, ("groups", "rows"), "feat", None),
            P(),
            P("section", None, None),
            P("section", None, None),
            P("section", None, None),
            P("section", None, None),
            P("section", None, None),
        ),
        out_specs=P("section", None, ("groups", "rows"), "feat", None),
        check_vma=False,
    )
```

time: 149 us -> 31.7 us (0.21); the launches traced: 147 us -> 31.5 us
  local copies, waits for them, and re-layouts: 65.1 us -> 1.88 us
  matrix products: 41.6 us -> 0 us
  Pallas kernels: 0 us -> 29.6 us
  blocking collectives: 25.8 us -> 0 us
  waiting for transfers between devices: 5.37 us -> 0 us
  other arithmetic: 4.52 us -> 0 us
  starting transfers between devices: 3.86 us -> 0 us
    dot_general x28 -> x0, matrix products: 31.9 us -> none  [the longest x4 7.15 us: per_device(): jnp.einsum('rhij,rjhd->rihd', weights, values, preferred_element_type=jnp...]
    reshape x28 -> x0, local copies, waits for them, and re-layouts: 31.2 us -> none  [the longest x4 7.3 us: per_device(): values = pairs[:, :, width:].reshape(test_n, groups, heads, head_dim)]
    pallas_call x0 -> x1, Pallas kernels: none -> 29.6 us  [per_device(): pl.pallas_call(functools.partial(kernel, sizes), out_shape=jax.ShapeDtype...]
    all_gather x5 -> x0, blocking collectives: 25.8 us -> none  [the longest x4 14.9 us: per_device(): pairs = lax.all_gather(qkv[:, :, width:], 'feat', axis=1, tiled=True)]
    sub x4 -> x0, matrix products: 9.65 us -> none  [per_device(): weights = jax.nn.softmax(scores, axis=-1).astype(jnp.bfloat16)]
    slice x18 -> x0, local copies, waits for them, and re-layouts: 9.32 us -> none  [the longest x4 3.22 us: per_device(): pairs = lax.all_gather(qkv[:, :, width:], 'feat', axis=1, tiled=True)]
    dot_general x8 -> x0, local copies, waits for them, and re-layouts: 8.43 us -> none  [the longest x4 5.67 us: per_device(): term = jnp.dot(item_mix, witem, preferred_element_type=jnp.float32)]
    ppermute x3 -> x0, waiting for transfers between devices: 5.37 us -> none  [from_behind(): return lax.ppermute(block, axis, route)]
  transfers between devices with their start and end apart: 3 -> 0, of which waited for: 3 -> 0; matrix products, arithmetic and copies ran while one was open for 7% -> 0% of each run, Pallas kernels for 0% -> 0%
where the time goes in v1:
time: 31.7 us; the launch traced here: 31.5 us
  Pallas kernels  29.6 us (93%)
  local copies, waits for them, and re-layouts  1.88 us (6%)
    pallas_call x1, Pallas kernels, per_device(): pl.pallas_call(functools.partial(kernel, sizes), out_shape=jax.ShapeDtype...  29.6 us
    unnamed x1, local copies, waits for them, and re-layouts  1.88 us

profile of v1, /device:TPU:3, one launch (start us, length us, event | category | flops | bytes accessed | tf_op | source)
XLA Modules:
  0.0 31.5 jit_solution(11458884769492660443)
XLA Ops:
  0.0 29.6 %shard_map.82 = bf16[1,3,32,4,512]{4,3,2,1,0:T(4,128)(2,1)} custom-call(bf16[3,32,4,512]{3,2,1,0:T(4,128)(2,1)} %rows_hbm.1, bf16[1,2,4,4,512]{4,3,2,1,0:T(4,128)(2,1)} %cache_hbm.1, s32[8,8]{1,0:T(8,128)} %pattern_ref.1, bf16[1,512,1536]{2,1,0:T(8,128)(2,1)} %qkv_hbm.1, bf16[1,512,512]{2,1,0:T(8,128)(2,1)} %out_hbm.1, bf16[1,512,512]{2,1,0:T(8,128)(2,1)} %query_hbm.1, ...), custom_call_target="tpu_custom_call" | custom-call | tf_op jit(solution)/shard_map/pallas_call | solution.py:279
  29.6 1.9 %copy.10 = bf16[1,3,32,4,512]{4,3,2,1,0:T(4,128)(2,1)} copy(bf16[1,3,32,4,512]{4,3,2,1,0:T(4,128)(2,1)} %shard_map.82) | data formatting | bytes 786432

commit v2 on v1

--- a/solution.py
+++ b/solution.py
@@ -33,9 +33,9 @@
 
 
 def kernel(
-    sizes, rows_hbm, cache_hbm, pattern_ref, qkv_hbm, out_hbm, query_hbm, item_hbm, gains_ref, hidden_hbm,
-    x_in, wqkv, wout, wquery, witem, h_buf, h_out, q_buf, kv_buf, cache_buf, k_stack, v_stack, feat_bias, item_bias, staged,
-    weight_sem, x_sem, own_sem, out_sem, kv_send, kv_recv, cache_send, cache_recv, h_send, h_recv,
+    sizes, rows_hbm, cache_hbm, pattern_ref, qkv_hbm, out_hbm, query_hbm, item_hbm, gains_ref, hidden_ref,
+    x_in, wqkv, wout, wquery, witem, h_buf, h_out, q_buf, kv_buf, cache_buf, k_stack, v_stack, feat_bias, item_bias,
+    weight_sem, x_sem, own_sem, kv_send, kv_recv, cache_send, cache_recv, h_send, h_recv,
 ):
     sections, row_devs = sizes
     micro, test_n, gd, width = x_in.shape
@@ -126,9 +126,6 @@
             send_sem=h_send.at[m], recv_sem=h_recv.at[m],
             device_id={"section": target}, device_id_type=MESH,
         )
-
-    def out_copy(m):
-        return pltpu.make_async_copy(staged.at[m], hidden_hbm.at[0, m], out_sem.at[m])
 
     groups = 2 * gd
     q_at = iota((half, groups), 0) % gd + feat * gd
@@ -147,6 +144,8 @@
         iota((tokens, 2 * nk), 0) % gd == iota((tokens, 2 * nk), 1) % gd, 0.0, EXCLUDED
     ).astype(F32)
 
+    low_lanes = iota((tokens, width), 1) % pair_w < pair_w // 2
+
     def project(m):
         @pl.when(first)
         def _():
@@ -161,7 +160,13 @@
         kv_buf[m, 0, :, :width] = dot(a, wqkv[:, width : 2 * width]).astype(BF16)
         kv_buf[m, 0, :, width:] = dot(a, wqkv[:, 2 * width :]).astype(BF16)
         kv_copy(m).start()
-        q_buf[m] = dot(a, wqkv[:, :width]).astype(BF16)
+        q = dot(a, wqkv[:, :width]) * factor
+        low = jnp.where(low_lanes, q, 0.0).astype(BF16)
+        high = jnp.where(low_lanes, 0.0, q).astype(BF16)
+        for block in range(2):
+            span = slice(block * half, (block + 1) * half)
+            q_buf[m, block, :half] = low[span]
+            q_buf[m, block, half:] = high[span]
 
     low_half = iota((half, pair_w), 1) < pair_w // 2
     ones = jnp.ones((2 * half, pair_w), BF16)
@@ -174,16 +179,15 @@
             for pair in range(pairs):
                 lanes = slice(pair * pair_w, (pair + 1) * pair_w)
                 v_lanes = slice(width + pair * pair_w, width + (pair + 1) * pair_w)
-                q = q_buf[m, span, lanes]
-                zero = jnp.zeros_like(q)
-                q2 = jnp.concatenate([jnp.where(low_half, q, zero), jnp.where(low_half, zero, q)], axis=0)
+                q2 = q_buf[m, block, :, lanes]
                 k = jnp.concatenate([kv_buf[m, 0, span, lanes], kv_buf[m, 1, span, lanes]], axis=0)
                 v = jnp.concatenate([kv_buf[m, 0, span, v_lanes], kv_buf[m, 1, span, v_lanes]], axis=0)
-                s = dot_t(q2, k) * factor + feat_bias[...]
+                s = dot_t(q2, k) + feat_bias[...]
                 p = jnp.exp2(s - jnp.max(s, axis=-1, keepdims=True)).astype(BF16)
                 o = dot(p, jnp.concatenate([v, ones], axis=1))
-                o = o[:, :pair_w] / o[:, pair_w:]
-                mixed.append(jnp.where(low_half, o[:half], o[half:]))
+                total = jnp.where(low_half, o[:half, pair_w:], o[half:, pair_w:])
+                o = jnp.where(low_half, o[:half, :pair_w], o[half:, :pair_w])
+                mixed.append(o * pl.reciprocal(total, approx=True))
             blocks.append(jnp.concatenate(mixed, axis=1))
         return jnp.concatenate(blocks, axis=0).astype(BF16)
 
@@ -193,12 +197,12 @@
         mixed = []
         for pair in range(pairs):
             lanes = slice(pair * pair_w, (pair + 1) * pair_w)
-            s = dot_t(query[:, lanes], k_stack[pair]) * factor + item_bias[...]
+            s = dot_t(query[:, lanes], k_stack[pair]) + item_bias[...]
             low = jnp.max(jnp.where(low_keys, s, -jnp.inf), axis=-1, keepdims=True)
             high = jnp.max(jnp.where(low_keys, -jnp.inf, s), axis=-1, keepdims=True)
             p = jnp.exp2(s - jnp.where(low_keys, low, high)).astype(BF16)
             o = dot(p, v_stack[pair])
-            mixed.append(o[:, :pair_w] / o[:, pair_w:])
+            mixed.append(o[:, :pair_w] * pl.reciprocal(o[:, pair_w:], approx=True))
         return jnp.concatenate(mixed, axis=1).astype(BF16)
 
     weights[0].wait()
@@ -238,7 +242,7 @@
 
         h1 = h_buf[m].astype(F32) + dot(mixed, wout[...])
         b = normed(h1, gains_ref[0, 1:2, :])
-        query = dot(b, wquery[...]).astype(BF16)
+        query = (dot(b, wquery[...]) * factor).astype(BF16)
         result = h1 + dot(item_mix(query), witem[...])
         h_out[m] = result.astype(BF16)
 
@@ -246,15 +250,13 @@
         def _():
             h_copy(m, section + 1).start()
 
-        staged[m] = result.reshape(test_n, gd, width).astype(BF16)
-        out_copy(m).start()
+        hidden_ref[0, m] = result.reshape(test_n, gd, width).astype(BF16)
         return carry
 
     lax.fori_loop(0, micro, step, 0)
 
     for m in range(micro):
         kv_copy(m).wait_send()
-        out_copy(m).wait()
 
     @pl.when(sends)
     def _():
@@ -273,14 +275,14 @@
     nk = row_devs * train_dev * gd
     pair_w = 2 * (width // HEADS)
     pairs = width // pair_w
-    anywhere = pl.BlockSpec(memory_space=pl.ANY)
+    anywhere = pl.BlockSpec(memory_space=pltpu.HBM)
     vmem = pl.BlockSpec(memory_space=pltpu.VMEM)
     dma = pltpu.SemaphoreType.DMA
     return pl.pallas_call(
         functools.partial(kernel, sizes),
         out_shape=jax.ShapeDtypeStruct((1, micro, test_n, gd, width), BF16),
         in_specs=[anywhere, anywhere, vmem, anywhere, anywhere, anywhere, anywhere, vmem],
-        out_specs=anywhere,
+        out_specs=vmem,
         scratch_shapes=[
             pltpu.VMEM((micro, test_n, gd, width), BF16),
             pltpu.VMEM((width, 3 * width), BF16),
@@ -289,18 +291,16 @@
             pltpu.VMEM((width, width), BF16),
             pltpu.VMEM((micro, tokens, width), BF16),
             pltpu.VMEM((micro, tokens, width), BF16),
-            pltpu.VMEM((micro, tokens, width), BF16),
+            pltpu.VMEM((micro, 2, tokens, width), BF16),
             pltpu.VMEM((micro, 2, tokens, 2 * width), BF16),
             pltpu.VMEM((row_devs, 2, train_dev, gd, width), BF16),
             pltpu.VMEM((pairs, 2 * nk, pair_w), BF16),
             pltpu.VMEM((pairs, 2 * nk, 2 * pair_w), BF16),
             pltpu.VMEM((tokens, tokens), F32),
             pltpu.VMEM((tokens, 2 * nk), F32),
-            pltpu.VMEM((micro, test_n, gd, width), BF16),
             dma((4,)),
             dma((micro,)),
             dma(()),
-            dma((micro,)),
             dma((micro,)),
             dma((micro,)),
             dma((row_devs - 1,)),
@@ -309,7 +309,7 @@
             dma((micro,)),
         ],
         compiler_params=pltpu.CompilerParams(
-            collective_id=0, has_side_effects=True, vmem_limit_bytes=60 * 1024 * 1024
+            collective_id=0, has_side_effects=True, vmem_limit_bytes=40 * 1024 * 1024
         ),
     )(test_rows, train_cache, pattern, feat_qkv, feat_out, item_query, item_out, gains)
 

time: 31.7 us -> 37.9 us (1.20)
  local copies, waits for them, and re-layouts: 1.88 us -> 8.4 us
  Pallas kernels: 29.6 us -> 29 us
    unnamed x1 -> x17, local copies, waits for them, and re-layouts: 1.88 us -> 8.4 us
    pallas_call x1, Pallas kernels: 29.6 us -> 29 us  [per_device(): pl.pallas_call(functools.partial(kernel, sizes), out_shape=jax.ShapeDtype...]
where the time goes in v2:
time: 37.9 us; the launch traced here: 37.4 us
  Pallas kernels  29 us (77%)
  local copies, waits for them, and re-layouts  8.4 us (22%)
    pallas_call x1, Pallas kernels, per_device(): pl.pallas_call(functools.partial(kernel, sizes), out_shape=jax.ShapeDtype...  29 us
    unnamed x17, local copies, waits for them, and re-layouts  8.4 us

profile of v2, /device:TPU:3, one launch (start us, length us, event | category | flops | bytes accessed | tf_op | source)
XLA Modules:
  0.0 37.4 jit_solution(12165773230806815001)
XLA Ops:
  0.0 0.0 copy-start
  0.0 1.4 %copy-done = bf16[1,512,1536]{2,1,0:T(8,128)(2,1)S(1)} copy-done((bf16[1,512,1536]{2,1,0:T(8,128)(2,1)S(1)}, bf16[1,512,1536]{2,1,0:T(8,128)(2,1)}, u32[]{:S(2)}) %copy-start) | copy-done | bytes 1572888
  1.4 0.0 copy-start.1
  1.4 1.0 %copy-done.1 = bf16[1,512,512]{2,1,0:T(8,128)(2,1)S(1)} copy-done((bf16[1,512,512]{2,1,0:T(8,128)(2,1)S(1)}, bf16[1,512,512]{2,1,0:T(8,128)(2,1)}, u32[]{:S(2)}) %copy-start.1) | copy-done | bytes 524312
  2.5 0.0 copy-start.2
  2.5 1.0 %copy-done.2 = bf16[1,512,512]{2,1,0:T(8,128)(2,1)S(1)} copy-done((bf16[1,512,512]{2,1,0:T(8,128)(2,1)S(1)}, bf16[1,512,512]{2,1,0:T(8,128)(2,1)}, u32[]{:S(2)}) %copy-start.2) | copy-done | bytes 524312
  3.5 0.0 copy-start.3
  3.5 1.0 %copy-done.3 = bf16[1,512,512]{2,1,0:T(8,128)(2,1)S(1)} copy-done((bf16[1,512,512]{2,1,0:T(8,128)(2,1)S(1)}, bf16[1,512,512]{2,1,0:T(8,128)(2,1)}, u32[]{:S(2)}) %copy-start.3) | copy-done | bytes 524312
  4.5 0.0 copy-start.4
  4.5 1.0 %copy-done.4 = bf16[3,32,4,512]{3,2,1,0:T(4,128)(2,1)S(1)} copy-done((bf16[3,32,4,512]{3,2,1,0:T(4,128)(2,1)S(1)}, bf16[3,32,4,512]{3,2,1,0:T(4,128)(2,1)}, u32[]{:S(2)}) %copy-start.4) | copy-done | bytes 393240
  5.5 0.0 copy-start.5
  5.5 0.8 %copy-done.5 = bf16[1,2,4,4,512]{4,3,2,1,0:T(4,128)(2,1)S(1)} copy-done((bf16[1,2,4,4,512]{4,3,2,1,0:T(4,128)(2,1)S(1)}, bf16[1,2,4,4,512]{4,3,2,1,0:T(4,128)(2,1)}, u32[]{:S(2)}) %copy-start.5) | copy-done | bytes 32792
  6.3 0.0 copy-start.6
  6.3 0.7 %copy-done.6 = s32[8,8]{1,0:T(8,128)S(1)} copy-done((s32[8,8]{1,0:T(8,128)S(1)}, s32[8,8]{1,0:T(8,128)}, u32[]{:S(2)}) %copy-start.6) | copy-done | bytes 280
  7.0 0.0 copy-start.7
  7.0 0.7 %copy-done.7 = f32[1,2,512]{2,1,0:T(2,128)S(1)} copy-done((f32[1,2,512]{2,1,0:T(2,128)S(1)}, f32[1,2,512]{2,1,0:T(2,128)}, u32[]{:S(2)}) %copy-start.7) | copy-done | bytes 4120
  7.7 29.0 %shard_map.82 = bf16[1,3,32,4,512]{4,3,2,1,0:T(4,128)(2,1)S(1)} custom-call(bf16[3,32,4,512]{3,2,1,0:T(4,128)(2,1)S(1)} %copy-done.4, bf16[1,2,4,4,512]{4,3,2,1,0:T(4,128)(2,1)S(1)} %copy-done.5, s32[8,8]{1,0:T(8,128)S(1)} %copy-done.6, bf16[1,512,1536]{2,1,0:T(8,128)(2,1)S(1)} %copy-done, bf16[1,512,512]{2,1,0:T(8,128)(2,1)S(1)} %copy-done.1, ...), custom_call_target="tpu_custom_call" | custom-call | tf_op jit(solution)/shard_map/pallas_call | solution.py:281
  36.7 0.7 %copy.10 = bf16[1,3,32,4,512]{4,3,2,1,0:T(4,128)(2,1)} copy(bf16[1,3,32,4,512]{4,3,2,1,0:T(4,128)(2,1)S(1)} %shard_map.82) | data formatting | bytes 786432
Async XLA Ops:
  0.0 1.4 %copy-start = (bf16[1,512,1536]{2,1,0:T(8,128)(2,1)S(1)}, bf16[1,512,1536]{2,1,0:T(8,128)(2,1)}, u32[]{:S(2)}) copy-start(bf16[1,512,1536]{2,1,0:T(8,128)(2,1)} %qkv_hbm.1) | copy-start | bytes 4718596
  1.4 1.0 %copy-start.1 = (bf16[1,512,512]{2,1,0:T(8,128)(2,1)S(1)}, bf16[1,512,512]{2,1,0:T(8,128)(2,1)}, u32[]{:S(2)}) copy-start(bf16[1,512,512]{2,1,0:T(8,128)(2,1)} %out_hbm.1) | copy-start | bytes 1572868
  2.5 1.0 %copy-start.2 = (bf16[1,512,512]{2,1,0:T(8,128)(2,1)S(1)}, bf16[1,512,512]{2,1,0:T(8,128)(2,1)}, u32[]{:S(2)}) copy-start(bf16[1,512,512]{2,1,0:T(8,128)(2,1)} %query_hbm.1) | copy-start | bytes 1572868
  3.5 1.0 %copy-start.3 = (bf16[1,512,512]{2,1,0:T(8,128)(2,1)S(1)}, bf16[1,512,512]{2,1,0:T(8,128)(2,1)}, u32[]{:S(2)}) copy-start(bf16[1,512,512]{2,1,0:T(8,128)(2,1)} %item_hbm.1) | copy-start | bytes 1572868
  4.5 1.0 %copy-start.4 = (bf16[3,32,4,512]{3,2,1,0:T(4,128)(2,1)S(1)}, bf16[3,32,4,512]{3,2,1,0:T(4,128)(2,1)}, u32[]{:S(2)}) copy-start(bf16[3,32,4,512]{3,2,1,0:T(4,128)(2,1)} %rows_hbm.1) | copy-start | bytes 1179652
  5.5 0.8 %copy-start.5 = (bf16[1,2,4,4,512]{4,3,2,1,0:T(4,128)(2,1)S(1)}, bf16[1,2,4,4,512]{4,3,2,1,0:T(4,128)(2,1)}, u32[]{:S(2)}) copy-start(bf16[1,2,4,4,512]{4,3,2,1,0:T(4,128)(2,1)} %cache_hbm.1) | copy-start | bytes 98308
  6.3 0.7 %copy-start.6 = (s32[8,8]{1,0:T(8,128)S(1)}, s32[8,8]{1,0:T(8,128)}, u32[]{:S(2)}) copy-start(s32[8,8]{1,0:T(8,128)} %pattern_ref.1) | copy-start | bytes 772
  7.0 0.7 %copy-start.7 = (f32[1,2,512]{2,1,0:T(2,128)S(1)}, f32[1,2,512]{2,1,0:T(2,128)}, u32[]{:S(2)}) copy-start(f32[1,2,512]{2,1,0:T(2,128)} %gains_ref.1) | copy-start | bytes 12292

commit v3 on v1

v3 whole, which is shorter than its diff:
```python
import functools
import math

import jax
import jax.numpy as jnp
from jax import lax
from jax.experimental import pallas as pl
from jax.experimental.pallas import tpu as pltpu
from jax.sharding import PartitionSpec as P

HEADS = 8
MESH = pl.DeviceIdType.MESH
F32 = jnp.float32
BF16 = jnp.bfloat16
EXCLUDED = -1e30


def iota(shape, dim):
    return lax.broadcasted_iota(jnp.int32, shape, dim)


def normed(x, gain):
    mean_sq = jnp.mean(x * x, axis=-1, keepdims=True)
    return (x * lax.rsqrt(mean_sq + 1e-06) * gain).astype(BF16)


def dot(a, b):
    return jnp.dot(a, b, preferred_element_type=F32)


def dot_t(a, b):
    return lax.dot_general(a, b, (((1,), (1,)), ((), ())), preferred_element_type=F32)


def kernel(
    sizes, rows_hbm, cache_hbm, pattern_ref, qkv_hbm, out_hbm, query_hbm, item_hbm, gains_ref, hidden_hbm,
    x_buf, wqkv, wout, wquery, witem, h_buf, h_out, cache_buf, k_stack, v_stack, feat_bias, item_bias, staged,
    weight_sem, x_sem, own_sem, out_sem, x_send, x_recv, cache_send, cache_recv, pass_send, pass_recv,
    h_send, h_recv, out_send, out_recv,
):
    sections, row_devs = sizes
    micro, feats, rows_n, gd, width = x_buf.shape
    half = rows_n * gd
    tokens = feats * half
    pair_w = 2 * (width // HEADS)
    pairs = width // pair_w
    train_dev = cache_buf.shape[3]
    nk = row_devs * train_dev * gd
    factor = math.log2(math.e) / math.sqrt(width // HEADS)

    section = lax.axis_index("section")
    row = lax.axis_index("rows")
    feat = lax.axis_index("feat")
    partner = 1 - feat
    first = section == 0
    receives = section > 0
    sends = section < sections - 1
    mine = pl.ds(feat * rows_n, rows_n)
    theirs = pl.ds(partner * rows_n, rows_n)

    weights = [
        pltpu.make_async_copy(src.at[0], dst, weight_sem.at[i])
        for i, (src, dst) in enumerate(
            [(qkv_hbm, wqkv), (out_hbm, wout), (query_hbm, wquery), (item_hbm, witem)]
        )
    ]

    def x_own(m):
        return pltpu.make_async_copy(rows_hbm.at[m, mine], x_buf.at[m, feat], x_sem.at[m])

    @pl.when(first)
    def _():
        for m in range(micro):
            x_own(m).start()

    for copy in weights:
        copy.start()
    own_cache = pltpu.make_async_copy(cache_hbm.at[0], cache_buf.at[feat, row], own_sem)
    own_cache.start()

    barrier = pltpu.get_barrier_semaphore()
    pl.semaphore_signal(barrier, inc=1, device_id={"feat": partner}, device_id_type=MESH)
    for off in range(1, row_devs):
        pl.semaphore_signal(
            barrier, inc=1, device_id={"rows": lax.rem(row + off, row_devs)}, device_id_type=MESH
        )

    @pl.when(receives)
    def _():
        pl.semaphore_signal(barrier, inc=1, device_id={"section": section - 1}, device_id_type=MESH)

    @pl.when(sends)
    def _():
        pl.semaphore_signal(barrier, inc=1, device_id={"section": section + 1}, device_id_type=MESH)

    pl.semaphore_wait(
        barrier, row_devs + jnp.where(receives, 1, 0) + jnp.where(sends, 1, 0)
    )

    def x_copy(m, source):
        return pltpu.make_async_remote_copy(
            src_ref=rows_hbm.at[m, theirs], dst_ref=x_buf.at[m, source],
            send_sem=x_send.at[m], recv_sem=x_recv.at[m],
            device_id={"feat": partner}, device_id_type=MESH,
        )

    def cache_copy(off):
        return pltpu.make_async_remote_copy(
            src_ref=cache_hbm.at[0], dst_ref=cache_buf.at[feat, row],
            send_sem=cache_send.at[off - 1], recv_sem=cache_recv.at[row],
            device_id={"rows": lax.rem(row + off, row_devs)}, device_id_type=MESH,
        )

    def cache_arrival(off):
        source = lax.rem(row + off, row_devs)
        return pltpu.make_async_remote_copy(
            src_ref=cache_hbm.at[0], dst_ref=cache_buf.at[feat, source],
            send_sem=cache_send.at[off - 1], recv_sem=cache_recv.at[source],
            device_id={"rows": source}, device_id_type=MESH,
        )

    def cache_pass(off, source_feat):
        source = lax.rem(row + off, row_devs)
        return pltpu.make_async_remote_copy(
            src_ref=cache_hbm.at[0] if off == 0 else cache_buf.at[feat, source],
            dst_ref=cache_buf.at[source_feat, source],
            send_sem=pass_send.at[off], recv_sem=pass_recv.at[off],
            device_id={"feat": partner}, device_id_type=MESH,
        )

    @pl.when(first)
    def _():
        x_copy(0, feat).start()

    for off in range(1, row_devs):
        cache_copy(off).start()

    @pl.when(first)
    def _():
        for m in range(1, micro):
            x_copy(m, feat).start()

    cache_pass(0, feat).start()

    def h_copy(m, target):
        return pltpu.make_async_remote_copy(
            src_ref=h_out.at[m], dst_ref=h_buf.at[m],
            send_sem=h_send.at[m], recv_sem=h_recv.at[m],
            device_id={"section": target}, device_id_type=MESH,
        )

    def out_own(m):
        return pltpu.make_async_copy(staged.at[m, feat], hidden_hbm.at[0, m, mine], out_sem.at[m])

    def out_copy(m, place):
        return pltpu.make_async_remote_copy(
            src_ref=staged.at[m, partner], dst_ref=hidden_hbm.at[0, m, place],
            send_sem=out_send.at[m], recv_sem=out_recv.at[m],
            device_id={"feat": partner}, device_id_type=MESH,
        )

    groups = feats * gd
    token = iota((tokens, groups), 0)
    pick_q = ((token // half) * gd + token % gd == iota((tokens, groups), 1)).astype(F32)
    token = iota((groups, tokens), 1)
    pick_k = ((token // half) * gd + token % gd == iota((groups, tokens), 0)).astype(F32)
    pattern = (pattern_ref[...] != 0).astype(F32)
    seen = dot(dot(pick_q, pattern), pick_k) > 0.5
    qi, ki = iota((tokens, tokens), 0), iota((tokens, tokens), 1)
    seen = (seen | (qi == ki)) & ((qi % half) // gd == (ki % half) // gd)
    bias = jnp.where(seen, 0.0, EXCLUDED).astype(F32)
    feat_bias[:tokens] = bias
    feat_bias[tokens:] = bias
    item_bias[...] = jnp.where(
        iota((half, 2 * nk), 0) % gd == iota((half, 2 * nk), 1) % gd, 0.0, EXCLUDED
    ).astype(F32)

    def pass_cache():
        for off in range(1, row_devs):
            cache_arrival(off).wait_recv()
            cache_pass(off, feat).start()

    def stack_cache():
        own_cache.wait()
        for off in range(row_devs):
            cache_pass(off, partner).wait_recv()
        side = iota((nk, pair_w), 1) < pair_w // 2
        one = jnp.where(side, 1.0, 0.0).astype(BF16)
        other = jnp.where(side, 0.0, 1.0).astype(BF16)
        for f in range(feats):
            for pair in range(pairs):
                lanes = slice(pair * pair_w, (pair + 1) * pair_w)
                k = cache_buf[f, :, 0, :, :, lanes].astype(F32).reshape(nk, pair_w)
                v = cache_buf[f, :, 1, :, :, lanes].astype(F32).reshape(nk, pair_w)
                k_stack[f, pair, :nk] = jnp.where(side, k, 0.0).astype(BF16)
                k_stack[f, pair, nk:] = jnp.where(side, 0.0, k).astype(BF16)
                v_stack[f, pair, :nk, :pair_w] = jnp.where(side, v, 0.0).astype(BF16)
                v_stack[f, pair, nk:, :pair_w] = jnp.where(side, 0.0, v).astype(BF16)
                v_stack[f, pair, :nk, pair_w:] = one
                v_stack[f, pair, nk:, pair_w:] = other

    low_half = iota((tokens, pair_w), 1) < pair_w // 2
    ones = jnp.ones((tokens, pair_w), BF16)

    def feature_mix(q, k, v):
        mixed = []
        for pair in range(pairs):
            lanes = slice(pair * pair_w, (pair + 1) * pair_w)
            q1 = q[:, lanes]
            q2 = jnp.concatenate(
                [jnp.where(low_half, q1, 0.0).astype(BF16), jnp.where(low_half, 0.0, q1).astype(BF16)], axis=0
            )
            s = dot_t(q2, k[:, lanes]) + feat_bias[...]
            p = jnp.exp2(s - jnp.max(s, axis=-1, keepdims=True)).astype(BF16)
            o = dot(p, jnp.concatenate([v[:, lanes], ones], axis=1))
            total = jnp.where(low_half, o[:tokens, pair_w:], o[tokens:, pair_w:])
            o = jnp.where(low_half, o[:tokens, :pair_w], o[tokens:, :pair_w])
            mixed.append((o * pl.reciprocal(total, approx=True)).astype(BF16))
        return jnp.concatenate(mixed, axis=1)

    low_keys = iota((half, 2 * nk), 1) < nk

    def item_mix(query):
        blocks = []
        for f in range(feats):
            mixed = []
            for pair in range(pairs):
                lanes = slice(pair * pair_w, (pair + 1) * pair_w)
                s = dot_t(query[f * half : (f + 1) * half, lanes], k_stack[f, pair]) + item_bias[...]
                low = jnp.max(jnp.where(low_keys, s, -jnp.inf), axis=-1, keepdims=True)
                high = jnp.max(jnp.where(low_keys, -jnp.inf, s), axis=-1, keepdims=True)
                p = jnp.exp2(s - jnp.where(low_keys, low, high)).astype(BF16)
                o = dot(p, v_stack[f, pair])
                mixed.append((o[:, :pair_w] * pl.reciprocal(o[:, pair_w:], approx=True)).astype(BF16))
            blocks.append(jnp.concatenate(mixed, axis=1))
        return jnp.concatenate(blocks, axis=0)

    @pl.when(receives)
    def _():
        pass_cache()
        stack_cache()

    weights[0].wait()
    weights[1].wait()
    weights[2].wait()
    weights[3].wait()

    def step(m, carry):
        @pl.when(first)
        def _():
            x_own(m).wait()
            x_copy(m, partner).wait_recv()
            h_buf[m] = x_buf[m].astype(F32).reshape(tokens, width).astype(BF16)

        @pl.when(receives)
        def _():
            h_copy(m, section - 1).wait_recv()

        h = h_buf[m].astype(F32)
        a = normed(h, gains_ref[0, 0:1, :])
        q = dot(a, wqkv[:, :width]) * factor
        k = dot(a, wqkv[:, width : 2 * width]).astype(BF16)
        v = dot(a, wqkv[:, 2 * width :]).astype(BF16)
        h1 = h + dot(feature_mix(q, k, v), wout[...])
        b = normed(h1, gains_ref[0, 1:2, :])
        query = (dot(b, wquery[...]) * factor).astype(BF16)

        @pl.when(first & (m == 0))
        def _():
            pass_cache()
            stack_cache()

        result = h1 + dot(item_mix(query), witem[...])
        h_out[m] = result.astype(BF16)

        @pl.when(sends)
        def _():
            h_copy(m, section + 1).start()

        staged[m] = result.reshape(feats, rows_n, gd, width).astype(BF16)
        out_copy(m, mine).start()
        out_own(m).start()
        return carry

    lax.fori_loop(0, micro, step, 0)

    for m in range(micro):
        out_own(m).wait()
        out_copy(m, theirs).wait()

    @pl.when(first)
    def _():
        for m in range(micro):
            x_copy(m, feat).wait_send()

    @pl.when(sends)
    def _():
        for m in range(micro):
            h_copy(m, section + 1).wait_send()

    for off in range(1, row_devs):
        cache_copy(off).wait_send()
    for off in range(row_devs):
        cache_pass(off, feat).wait_send()


def per_device(sizes, test_rows, train_cache, pattern, feat_qkv, feat_out, item_query, item_out, gains):
    sections, row_devs = sizes
    micro, test_n, gd, width = test_rows.shape
    train_dev = train_cache.shape[2]
    feats = 2
    rows_n = test_n // feats
    tokens = test_n * gd
    nk = row_devs * train_dev * gd
    pair_w = 2 * (width // HEADS)
    pairs = width // pair_w
    anywhere = pl.BlockSpec(memory_space=pl.ANY)
    vmem = pl.BlockSpec(memory_space=pltpu.VMEM)
    dma = pltpu.SemaphoreType.DMA
    return pl.pallas_call(
        functools.partial(kernel, sizes),
        out_shape=jax.ShapeDtypeStruct((1, micro, test_n, gd, width), BF16),
        in_specs=[anywhere, anywhere, vmem, anywhere, anywhere, anywhere, anywhere, vmem],
        out_specs=anywhere,
        scratch_shapes=[
            pltpu.VMEM((micro, feats, rows_n, gd, width), BF16),
            pltpu.VMEM((width, 3 * width), BF16),
            pltpu.VMEM((width, width), BF16),
            pltpu.VMEM((width, width), BF16),
            pltpu.VMEM((width, width), BF16),
            pltpu.VMEM((micro, tokens, width), BF16),
            pltpu.VMEM((micro, tokens, width), BF16),
            pltpu.VMEM((feats, row_devs, 2, train_dev, gd, width), BF16),
            pltpu.VMEM((feats, pairs, 2 * nk, pair_w), BF16),
            pltpu.VMEM((feats, pairs, 2 * nk, 2 * pair_w), BF16),
            pltpu.VMEM((2 * tokens, tokens), F32),
            pltpu.VMEM((tokens // feats, 2 * nk), F32),
            pltpu.VMEM((micro, feats, rows_n, gd, width), BF16),
            dma((4,)),
            dma((micro,)),
            dma(()),
            dma((micro,)),
            dma((micro,)),
            dma((micro,)),
            dma((row_devs - 1,)),
            dma((row_devs,)),
            dma((row_devs,)),
            dma((row_devs,)),
            dma((micro,)),
            dma((micro,)),
            dma((micro,)),
            dma((micro,)),
        ],
        compiler_params=pltpu.CompilerParams(
            collective_id=0, has_side_effects=True, vmem_limit_bytes=60 * 1024 * 1024
        ),
    )(test_rows, train_cache, pattern, feat_qkv, feat_out, item_query, item_out, gains)


def solution(mesh):
    sizes = (mesh.shape["section"], mesh.shape["rows"])
    return jax.shard_map(
        functools.partial(per_device, sizes),
        mesh=mesh,
        in_specs=(
            P(None, ("groups", "rows"), "feat", None),
            P("section", None, ("groups", "rows"), "feat", None),
            P(),
            P("section", None, None),
            P("section", None, None),
            P("section", None, None),
            P("section", None, None),
            P("section", None, None),
        ),
        out_specs=P("section", None, ("groups", "rows"), "feat", None),
        check_vma=False,
    )
```

time: 31.7 us -> 29.4 us (0.927)
  Pallas kernels: 29.6 us -> 27.3 us
    pallas_call x1, Pallas kernels: 29.6 us -> 27.3 us  [per_device(): pl.pallas_call(functools.partial(kernel, sizes), out_shape=jax.ShapeDtype...]
where the time goes in v3:
time: 29.4 us; the launch traced here: 29.2 us
  Pallas kernels  27.3 us (93%)
  local copies, waits for them, and re-layouts  1.88 us (6%)
    pallas_call x1, Pallas kernels, per_device(): pl.pallas_call(functools.partial(kernel, sizes), out_shape=jax.ShapeDtype...  27.3 us
    unnamed x1, local copies, waits for them, and re-layouts  1.88 us

profile of v3, /device:TPU:3, one launch (start us, length us, event | category | flops | bytes accessed | tf_op | source)
XLA Modules:
  0.0 29.2 jit_solution(17092576411801317814)
XLA Ops:
  0.0 27.3 %shard_map.82 = bf16[1,3,32,4,512]{4,3,2,1,0:T(4,128)(2,1)} custom-call(bf16[3,32,4,512]{3,2,1,0:T(4,128)(2,1)} %rows_hbm.1, bf16[1,2,4,4,512]{4,3,2,1,0:T(4,128)(2,1)} %cache_hbm.1, s32[8,8]{1,0:T(8,128)} %pattern_ref.1, bf16[1,512,1536]{2,1,0:T(8,128)(2,1)} %qkv_hbm.1, bf16[1,512,512]{2,1,0:T(8,128)(2,1)} %out_hbm.1, bf16[1,512,512]{2,1,0:T(8,128)(2,1)} %query_hbm.1, ...), custom_call_target="tpu_custom_call" | custom-call | tf_op jit(solution)/shard_map/pallas_call | solution.py:320
  27.3 1.9 %copy.10 = bf16[1,3,32,4,512]{4,3,2,1,0:T(4,128)(2,1)} copy(bf16[1,3,32,4,512]{4,3,2,1,0:T(4,128)(2,1)} %shard_map.82) | data formatting | bytes 786432

commit v4 on v3

--- a/solution.py
+++ b/solution.py
@@ -34,7 +34,7 @@
 
 def kernel(
     sizes, rows_hbm, cache_hbm, pattern_ref, qkv_hbm, out_hbm, query_hbm, item_hbm, gains_ref, hidden_hbm,
-    x_buf, wqkv, wout, wquery, witem, h_buf, h_out, cache_buf, k_stack, v_stack, feat_bias, item_bias, staged,
+    x_buf, wqkv, wout, wquery, witem, h_buf, h_out, h1_buf, query_buf, cache_buf, k_stack, v_stack, feat_bias, item_bias, staged,
     weight_sem, x_sem, own_sem, out_sem, x_send, x_recv, cache_send, cache_recv, pass_send, pass_recv,
     h_send, h_recv, out_send, out_recv,
 ):
@@ -240,37 +240,42 @@
         pass_cache()
         stack_cache()
 
-    weights[0].wait()
-    weights[1].wait()
-    weights[2].wait()
-    weights[3].wait()
-
-    def step(m, carry):
-        @pl.when(first)
-        def _():
-            x_own(m).wait()
-            x_copy(m, partner).wait_recv()
-            h_buf[m] = x_buf[m].astype(F32).reshape(tokens, width).astype(BF16)
-
-        @pl.when(receives)
-        def _():
-            h_copy(m, section - 1).wait_recv()
-
-        h = h_buf[m].astype(F32)
+    for copy in weights:
+        copy.wait()
+
+    def feature_half(places):
+        count = len(places) * tokens
+        h = jnp.concatenate([h_buf[m] for m in places], axis=0).astype(F32)
         a = normed(h, gains_ref[0, 0:1, :])
         q = dot(a, wqkv[:, :width]) * factor
         k = dot(a, wqkv[:, width : 2 * width]).astype(BF16)
         v = dot(a, wqkv[:, 2 * width :]).astype(BF16)
-        h1 = h + dot(feature_mix(q, k, v), wout[...])
+        spans = [slice(at, at + tokens) for at in range(0, count, tokens)]
+        mixed = jnp.concatenate([feature_mix(q[at], k[at], v[at]) for at in spans], axis=0)
+        h1 = h + dot(mixed, wout[...])
         b = normed(h1, gains_ref[0, 1:2, :])
         query = (dot(b, wquery[...]) * factor).astype(BF16)
-
-        @pl.when(first & (m == 0))
+        for m, at in zip(places, spans):
+            h1_buf[m] = h1[at]
+            query_buf[m] = query[at]
+
+    @pl.when(first)
+    def _():
+        for m in range(micro):
+            x_own(m).wait()
+            x_copy(m, partner).wait_recv()
+            h_buf[m] = x_buf[m].astype(F32).reshape(tokens, width).astype(BF16)
+        pass_cache()
+        feature_half(range(micro))
+        stack_cache()
+
+    def step(m, carry):
+        @pl.when(receives)
         def _():
-            pass_cache()
-            stack_cache()
-
-        result = h1 + dot(item_mix(query), witem[...])
+            h_copy(m, section - 1).wait_recv()
+            feature_half([m])
+
+        result = h1_buf[m] + dot(item_mix(query_buf[m]), witem[...])
         h_out[m] = result.astype(BF16)
 
         @pl.when(sends)
@@ -302,6 +307,17 @@
         cache_copy(off).wait_send()
     for off in range(row_devs):
         cache_pass(off, feat).wait_send()
+
+
+def hand_over(source, target, sem):
+    copies = [
+        pltpu.make_async_copy(source.at[0, m], target.at[0, m], sem.at[m])
+        for m in range(source.shape[1])
+    ]
+    for copy in copies:
+        copy.start()
+    for copy in copies:
+        copy.wait()
 
 
 def per_device(sizes, test_rows, train_cache, pattern, feat_qkv, feat_out, item_query, item_out, gains):
@@ -317,7 +333,7 @@
     anywhere = pl.BlockSpec(memory_space=pl.ANY)
     vmem = pl.BlockSpec(memory_space=pltpu.VMEM)
     dma = pltpu.SemaphoreType.DMA
-    return pl.pallas_call(
+    hidden = pl.pallas_call(
         functools.partial(kernel, sizes),
         out_shape=jax.ShapeDtypeStruct((1, micro, test_n, gd, width), BF16),
         in_specs=[anywhere, anywhere, vmem, anywhere, anywhere, anywhere, anywhere, vmem],
@@ -330,6 +346,8 @@
             pltpu.VMEM((width, width), BF16),
             pltpu.VMEM((micro, tokens, width), BF16),
             pltpu.VMEM((micro, tokens, width), BF16),
+            pltpu.VMEM((micro, tokens, width), F32),
+            pltpu.VMEM((micro, tokens, width), BF16),
             pltpu.VMEM((feats, row_devs, 2, train_dev, gd, width), BF16),
             pltpu.VMEM((feats, pairs, 2 * nk, pair_w), BF16),
             pltpu.VMEM((feats, pairs, 2 * nk, 2 * pair_w), BF16),
@@ -355,6 +373,13 @@
             collective_id=0, has_side_effects=True, vmem_limit_bytes=60 * 1024 * 1024
         ),
     )(test_rows, train_cache, pattern, feat_qkv, feat_out, item_query, item_out, gains)
+    return pl.pallas_call(
+        hand_over,
+        out_shape=jax.ShapeDtypeStruct(hidden.shape, hidden.dtype),
+        in_specs=[anywhere],
+        out_specs=anywhere,
+        scratch_shapes=[dma((micro,))],
+    )(hidden)
 
 
 def solution(mesh):

time: 29.4 us -> 44.3 us (1.51)
  Pallas kernels: 27.3 us -> 44.1 us
  local copies, waits for them, and re-layouts: 1.88 us -> 0 us
    pallas_call x0 -> x1, Pallas kernels: none -> 13 us  [per_device(): pl.pallas_call(hand_over, out_shape=jax.ShapeDtypeStruct(hidden.shape, hi...]
    pallas_call x1, Pallas kernels: 27.3 us -> 31 us  [per_device(): pl.pallas_call(functools.partial(kernel, sizes), out_shape=jax.ShapeDtype...]
    unnamed x1 -> x0, local copies, waits for them, and re-layouts: 1.88 us -> none
where the time goes in v4:
time: 44.3 us; the launch traced here: 44.1 us
  Pallas kernels  44.1 us (100%)
    pallas_call x1, Pallas kernels, per_device(): pl.pallas_call(functools.partial(kernel, sizes), out_shape=jax.ShapeDtype...  31 us
    pallas_call x1, Pallas kernels, per_device(): pl.pallas_call(hand_over, out_shape=jax.ShapeDtypeStruct(hidden.shape, hi...  13 us

profile of v4, /device:TPU:3, one launch (start us, length us, event | category | flops | bytes accessed | tf_op | source)
XLA Modules:
  0.0 44.1 jit_solution(1706899121014239008)
XLA Ops:
  0.0 31.0 %shard_map.82.source = bf16[1,3,32,4,512]{4,3,2,1,0:T(4,128)(2,1)} custom-call(bf16[3,32,4,512]{3,2,1,0:T(4,128)(2,1)} %rows_hbm.1, bf16[1,2,4,4,512]{4,3,2,1,0:T(4,128)(2,1)} %cache_hbm.1, s32[8,8]{1,0:T(8,128)} %pattern_ref.1, bf16[1,512,1536]{2,1,0:T(8,128)(2,1)} %qkv_hbm.1, bf16[1,512,512]{2,1,0:T(8,128)(2,1)} %out_hbm.1, ...), custom_call_target="tpu_custom_call" | custom-call | tf_op jit(solution)/shard_map/pallas_call | solution.py:336
  31.0 13.0 %shard_map.83 = bf16[1,3,32,4,512]{4,3,2,1,0:T(4,128)(2,1)} custom-call(bf16[1,3,32,4,512]{4,3,2,1,0:T(4,128)(2,1)} %shard_map.82.source), custom_call_target="tpu_custom_call" | custom-call | tf_op jit(solution)/shard_map/pallas_call | solution.py:376

commit v5 on v3

--- a/solution.py
+++ b/solution.py
@@ -34,18 +34,21 @@
 
 def kernel(
     sizes, rows_hbm, cache_hbm, pattern_ref, qkv_hbm, out_hbm, query_hbm, item_hbm, gains_ref, hidden_hbm,
-    x_buf, wqkv, wout, wquery, witem, h_buf, h_out, cache_buf, k_stack, v_stack, feat_bias, item_bias, staged,
+    x_buf, wqkv, wout, wquery, witem, h_buf, h_out, cache_buf, k_stack, v_stack, feat_bias, item_bias, staged, wide, cache_wide,
     weight_sem, x_sem, own_sem, out_sem, x_send, x_recv, cache_send, cache_recv, pass_send, pass_recv,
     h_send, h_recv, out_send, out_recv,
 ):
     sections, row_devs = sizes
-    micro, feats, rows_n, gd, width = x_buf.shape
-    half = rows_n * gd
-    tokens = feats * half
+    micro, tokens, width = h_buf.shape
+    feats = x_buf.shape[1]
     pair_w = 2 * (width // HEADS)
     pairs = width // pair_w
-    train_dev = cache_buf.shape[3]
-    nk = row_devs * train_dev * gd
+    half = tokens // feats
+    gd = pattern_ref.shape[0] // feats
+    rows_n = half // gd
+    per_row = gd * pairs
+    train_n = cache_wide.shape[0] // per_row
+    nk = train_n * gd
     factor = math.log2(math.e) / math.sqrt(width // HEADS)
 
     section = lax.axis_index("section")
@@ -55,8 +58,9 @@
     first = section == 0
     receives = section > 0
     sends = section < sections - 1
-    mine = pl.ds(feat * rows_n, rows_n)
-    theirs = pl.ds(partner * rows_n, rows_n)
+    block_n = rows_n * per_row
+    mine = pl.ds(feat * block_n, block_n)
+    theirs = pl.ds(partner * block_n, block_n)
 
     weights = [
         pltpu.make_async_copy(src.at[0], dst, weight_sem.at[i])
@@ -160,19 +164,17 @@
         )
 
     groups = feats * gd
-    token = iota((tokens, groups), 0)
-    pick_q = ((token // half) * gd + token % gd == iota((tokens, groups), 1)).astype(F32)
-    token = iota((groups, tokens), 1)
-    pick_k = ((token // half) * gd + token % gd == iota((groups, tokens), 0)).astype(F32)
+    pick_q = (iota((tokens, groups), 0) // rows_n == iota((tokens, groups), 1)).astype(F32)
+    pick_k = (iota((groups, tokens), 1) // rows_n == iota((groups, tokens), 0)).astype(F32)
     pattern = (pattern_ref[...] != 0).astype(F32)
     seen = dot(dot(pick_q, pattern), pick_k) > 0.5
     qi, ki = iota((tokens, tokens), 0), iota((tokens, tokens), 1)
-    seen = (seen | (qi == ki)) & ((qi % half) // gd == (ki % half) // gd)
+    seen = (seen | (qi == ki)) & (qi % rows_n == ki % rows_n)
     bias = jnp.where(seen, 0.0, EXCLUDED).astype(F32)
     feat_bias[:tokens] = bias
     feat_bias[tokens:] = bias
     item_bias[...] = jnp.where(
-        iota((half, 2 * nk), 0) % gd == iota((half, 2 * nk), 1) % gd, 0.0, EXCLUDED
+        iota((half, 2 * nk), 0) // rows_n == (iota((half, 2 * nk), 1) % nk) // train_n, 0.0, EXCLUDED
     ).astype(F32)
 
     def pass_cache():
@@ -188,16 +190,22 @@
         one = jnp.where(side, 1.0, 0.0).astype(BF16)
         other = jnp.where(side, 0.0, 1.0).astype(BF16)
         for f in range(feats):
-            for pair in range(pairs):
-                lanes = slice(pair * pair_w, (pair + 1) * pair_w)
-                k = cache_buf[f, :, 0, :, :, lanes].astype(F32).reshape(nk, pair_w)
-                v = cache_buf[f, :, 1, :, :, lanes].astype(F32).reshape(nk, pair_w)
-                k_stack[f, pair, :nk] = jnp.where(side, k, 0.0).astype(BF16)
-                k_stack[f, pair, nk:] = jnp.where(side, 0.0, k).astype(BF16)
-                v_stack[f, pair, :nk, :pair_w] = jnp.where(side, v, 0.0).astype(BF16)
-                v_stack[f, pair, nk:, :pair_w] = jnp.where(side, 0.0, v).astype(BF16)
-                v_stack[f, pair, :nk, pair_w:] = one
-                v_stack[f, pair, nk:, pair_w:] = other
+            for kind in range(2):
+                cache_wide[...] = cache_buf[f, :, kind].astype(F32).reshape(cache_wide.shape)
+                for pair in range(pairs):
+                    part = jnp.concatenate(
+                        [cache_wide[pl.ds(pair * gd + g, train_n, stride=per_row), :] for g in range(gd)], axis=0
+                    )
+                    low = jnp.where(side, part, 0.0).astype(BF16)
+                    high = jnp.where(side, 0.0, part).astype(BF16)
+                    if kind == 0:
+                        k_stack[f, pair, :nk] = low
+                        k_stack[f, pair, nk:] = high
+                    else:
+                        v_stack[f, pair, :nk, :pair_w] = low
+                        v_stack[f, pair, nk:, :pair_w] = high
+                        v_stack[f, pair, :nk, pair_w:] = one
+                        v_stack[f, pair, nk:, pair_w:] = other
 
     low_half = iota((tokens, pair_w), 1) < pair_w // 2
     ones = jnp.ones((tokens, pair_w), BF16)
@@ -245,12 +253,23 @@
     weights[2].wait()
     weights[3].wait()
 
+    def spread(pair):
+        return [
+            pl.ds(f * block_n + pair * gd + g, rows_n, stride=per_row)
+            for f in range(feats)
+            for g in range(gd)
+        ]
+
     def step(m, carry):
         @pl.when(first)
         def _():
             x_own(m).wait()
             x_copy(m, partner).wait_recv()
-            h_buf[m] = x_buf[m].astype(F32).reshape(tokens, width).astype(BF16)
+            wide[...] = x_buf[m].astype(F32).reshape(wide.shape)
+            for pair in range(pairs):
+                part = [wide[place, :] for place in spread(pair)]
+                lanes = slice(pair * pair_w, (pair + 1) * pair_w)
+                h_buf[m, :, lanes] = jnp.concatenate(part, axis=0).astype(BF16)
 
         @pl.when(receives)
         def _():
@@ -277,7 +296,10 @@
         def _():
             h_copy(m, section + 1).start()
 
-        staged[m] = result.reshape(feats, rows_n, gd, width).astype(BF16)
+        for pair in range(pairs):
+            for at, place in enumerate(spread(pair)):
+                wide[place, :] = result[at * rows_n : (at + 1) * rows_n, pair * pair_w : (pair + 1) * pair_w]
+        staged[m] = wide[...].reshape(feats, block_n, pair_w).astype(BF16)
         out_copy(m, mine).start()
         out_own(m).start()
         return carry
@@ -302,6 +324,22 @@
         cache_copy(off).wait_send()
     for off in range(row_devs):
         cache_pass(off, feat).wait_send()
+
+
+def hand_over(source, target, sem):
+    micro, parts = sem.shape
+    piece = source.shape[2] // parts
+    copies = []
+    for m in range(micro):
+        for part in range(parts):
+            span = pl.ds(part * piece, piece)
+            copies.append(
+                pltpu.make_async_copy(source.at[0, m, span], target.at[0, m, span], sem.at[m, part])
+            )
+    for copy in copies:
+        copy.start()
+    for copy in copies:
+        copy.wait()
 
 
 def per_device(sizes, test_rows, train_cache, pattern, feat_qkv, feat_out, item_query, item_out, gains):
@@ -317,25 +355,33 @@
     anywhere = pl.BlockSpec(memory_space=pl.ANY)
     vmem = pl.BlockSpec(memory_space=pltpu.VMEM)
     dma = pltpu.SemaphoreType.DMA
-    return pl.pallas_call(
+    per_row = gd * pairs
+
+    def as_rows(x):
+        pieces = x.reshape(x.shape[:-1] + (pairs, pair_w)).swapaxes(-3, -2)
+        return pieces.reshape(x.shape[:-3] + (x.shape[-3] * per_row, pair_w))
+
+    hidden = pl.pallas_call(
         functools.partial(kernel, sizes),
-        out_shape=jax.ShapeDtypeStruct((1, micro, test_n, gd, width), BF16),
+        out_shape=jax.ShapeDtypeStruct((1, micro, test_n * per_row, pair_w), BF16),
         in_specs=[anywhere, anywhere, vmem, anywhere, anywhere, anywhere, anywhere, vmem],
         out_specs=anywhere,
         scratch_shapes=[
-            pltpu.VMEM((micro, feats, rows_n, gd, width), BF16),
+            pltpu.VMEM((micro, feats, rows_n * per_row, pair_w), BF16),
             pltpu.VMEM((width, 3 * width), BF16),
             pltpu.VMEM((width, width), BF16),
             pltpu.VMEM((width, width), BF16),
             pltpu.VMEM((width, width), BF16),
             pltpu.VMEM((micro, tokens, width), BF16),
             pltpu.VMEM((micro, tokens, width), BF16),
-            pltpu.VMEM((feats, row_devs, 2, train_dev, gd, width), BF16),
+            pltpu.VMEM((feats, row_devs, 2, train_dev * per_row, pair_w), BF16),
             pltpu.VMEM((feats, pairs, 2 * nk, pair_w), BF16),
             pltpu.VMEM((feats, pairs, 2 * nk, 2 * pair_w), BF16),
             pltpu.VMEM((2 * tokens, tokens), F32),
             pltpu.VMEM((tokens // feats, 2 * nk), F32),
-            pltpu.VMEM((micro, feats, rows_n, gd, width), BF16),
+            pltpu.VMEM((micro, feats, rows_n * per_row, pair_w), BF16),
+            pltpu.VMEM((test_n * per_row, pair_w), F32),
+            pltpu.VMEM((row_devs * train_dev * per_row, pair_w), F32),
             dma((4,)),
             dma((micro,)),
             dma(()),
@@ -354,7 +400,17 @@
         compiler_params=pltpu.CompilerParams(
             collective_id=0, has_side_effects=True, vmem_limit_bytes=60 * 1024 * 1024
         ),
-    )(test_rows, train_cache, pattern, feat_qkv, feat_out, item_query, item_out, gains)
+    )(as_rows(test_rows), as_rows(train_cache), pattern, feat_qkv, feat_out, item_query, item_out, gains)
+    hidden = pl.pallas_call(
+        hand_over,
+        out_shape=jax.ShapeDtypeStruct(hidden.shape, hidden.dtype),
+        in_specs=[anywhere],
+        out_specs=anywhere,
+        scratch_shapes=[dma((micro, 4))],
+        compiler_params=pltpu.CompilerParams(vmem_limit_bytes=60 * 1024 * 1024),
+    )(hidden)
+    hidden = hidden.reshape(1, micro, test_n, pairs, gd, pair_w).swapaxes(-3, -2)
+    return hidden.reshape(1, micro, test_n, gd, width)
 
 
 def solution(mesh):

time: 29.4 us -> 41.2 us (1.40)
  Pallas kernels: 27.3 us -> 41 us
  local copies, waits for them, and re-layouts: 1.88 us -> 0 us
    pallas_call x0 -> x1, Pallas kernels: none -> 13.1 us  [per_device(): pl.pallas_call(hand_over, out_shape=jax.ShapeDtypeStruct(hidden.shape, hi...]
    unnamed x1 -> x0, local copies, waits for them, and re-layouts: 1.88 us -> none
    pallas_call x1, Pallas kernels: 27.3 us -> 27.8 us  [per_device(): pl.pallas_call(functools.partial(kernel, sizes), out_shape=jax.ShapeDtype...]
where the time goes in v5:
time: 41.2 us; the launch traced here: 41 us
  Pallas kernels  41 us (100%)
    pallas_call x1, Pallas kernels, per_device(): pl.pallas_call(functools.partial(kernel, sizes), out_shape=jax.ShapeDtype...  27.8 us
    pallas_call x1, Pallas kernels, per_device(): pl.pallas_call(hand_over, out_shape=jax.ShapeDtypeStruct(hidden.shape, hi...  13.1 us

profile of v5, /device:TPU:3, one launch (start us, length us, event | category | flops | bytes accessed | tf_op | source)
XLA Modules:
  0.0 41.0 jit_solution(13188591929405075117)
XLA Ops:
  0.0 27.8 %shard_map.82.source = bf16[1,3,512,128]{3,2,1,0:T(8,128)(2,1)} custom-call(bf16[3,512,128]{2,1,0:T(8,128)(2,1)} %bitcast.15, bf16[1,2,64,128]{3,2,1,0:T(8,128)(2,1)} %bitcast.16, s32[8,8]{1,0:T(8,128)} %pattern_ref.1, bf16[1,512,1536]{2,1,0:T(8,128)(2,1)} %qkv_hbm.1, bf16[1,512,512]{2,1,0:T(8,128)(2,1)} %out_hbm.1, bf16[1,512,512]{2,1,0:T(8,128)(2,1)} %query_hbm.1, ...), custom_call_target="tpu_custom_call" | custom-call | tf_op jit(solution)/shard_map/pallas_call | solution.py:364
  27.9 13.1 %shard_map.83 = bf16[1,3,512,128]{3,2,1,0:T(8,128)(2,1)} custom-call(bf16[1,3,512,128]{3,2,1,0:T(8,128)(2,1)} %shard_map.82.source), custom_call_target="tpu_custom_call" | custom-call | tf_op jit(solution)/shard_map/pallas_call | solution.py:404

commit v6 on v5

--- a/solution.py
+++ b/solution.py
@@ -34,7 +34,7 @@
 
 def kernel(
     sizes, rows_hbm, cache_hbm, pattern_ref, qkv_hbm, out_hbm, query_hbm, item_hbm, gains_ref, hidden_hbm,
-    x_buf, wqkv, wout, wquery, witem, h_buf, h_out, cache_buf, k_stack, v_stack, feat_bias, item_bias, staged, wide, cache_wide,
+    x_buf, wqkv, wout, wquery, witem, h_buf, h_out, cache_buf, k_stack, v_stack, feat_bias, item_bias, staged, wide, cache_wide, qkv, mix, query, h1_buf,
     weight_sem, x_sem, own_sem, out_sem, x_send, x_recv, cache_send, cache_recv, pass_send, pass_recv,
     h_send, h_recv, out_send, out_recv,
 ):
@@ -189,59 +189,70 @@
         side = iota((nk, pair_w), 1) < pair_w // 2
         one = jnp.where(side, 1.0, 0.0).astype(BF16)
         other = jnp.where(side, 0.0, 1.0).astype(BF16)
-        for f in range(feats):
-            for kind in range(2):
-                cache_wide[...] = cache_buf[f, :, kind].astype(F32).reshape(cache_wide.shape)
-                for pair in range(pairs):
-                    part = jnp.concatenate(
-                        [cache_wide[pl.ds(pair * gd + g, train_n, stride=per_row), :] for g in range(gd)], axis=0
-                    )
-                    low = jnp.where(side, part, 0.0).astype(BF16)
-                    high = jnp.where(side, 0.0, part).astype(BF16)
-                    if kind == 0:
-                        k_stack[f, pair, :nk] = low
-                        k_stack[f, pair, nk:] = high
-                    else:
-                        v_stack[f, pair, :nk, :pair_w] = low
-                        v_stack[f, pair, nk:, :pair_w] = high
-                        v_stack[f, pair, :nk, pair_w:] = one
-                        v_stack[f, pair, nk:, pair_w:] = other
+        def one_kind(f, kind, store):
+            cache_wide[...] = cache_buf[f, :, kind].astype(F32).reshape(cache_wide.shape)
+            for pair in range(pairs):
+                part = jnp.concatenate(
+                    [cache_wide[pl.ds(pair * gd + g, train_n, stride=per_row), :] for g in range(gd)], axis=0
+                )
+                store(pair, jnp.where(side, part, 0.0).astype(BF16), jnp.where(side, 0.0, part).astype(BF16))
+
+        def one_feat(f, carry):
+            def keys(pair, low, high):
+                k_stack[f, pair, :nk] = low
+                k_stack[f, pair, nk:] = high
+
+            def values(pair, low, high):
+                v_stack[f, pair, :nk, :pair_w] = low
+                v_stack[f, pair, nk:, :pair_w] = high
+                v_stack[f, pair, :nk, pair_w:] = one
+                v_stack[f, pair, nk:, pair_w:] = other
+
+            one_kind(f, 0, keys)
+            one_kind(f, 1, values)
+            return carry
+
+        lax.fori_loop(0, feats, one_feat, 0)
 
     low_half = iota((tokens, pair_w), 1) < pair_w // 2
     ones = jnp.ones((tokens, pair_w), BF16)
 
-    def feature_mix(q, k, v):
-        mixed = []
-        for pair in range(pairs):
-            lanes = slice(pair * pair_w, (pair + 1) * pair_w)
-            q1 = q[:, lanes]
+    def lanes_of(pair, offset=0):
+        return pl.ds(pl.multiple_of(offset + pair * pair_w, pair_w), pair_w)
+
+    def feature_mix():
+        def one_pair(pair, carry):
+            q1 = qkv[:, lanes_of(pair)] * factor
+            k = qkv[:, lanes_of(pair, width)].astype(BF16)
+            v = qkv[:, lanes_of(pair, 2 * width)].astype(BF16)
             q2 = jnp.concatenate(
                 [jnp.where(low_half, q1, 0.0).astype(BF16), jnp.where(low_half, 0.0, q1).astype(BF16)], axis=0
             )
-            s = dot_t(q2, k[:, lanes]) + feat_bias[...]
+            s = dot_t(q2, k) + feat_bias[...]
             p = jnp.exp2(s - jnp.max(s, axis=-1, keepdims=True)).astype(BF16)
-            o = dot(p, jnp.concatenate([v[:, lanes], ones], axis=1))
+            o = dot(p, jnp.concatenate([v, ones], axis=1))
             total = jnp.where(low_half, o[:tokens, pair_w:], o[tokens:, pair_w:])
             o = jnp.where(low_half, o[:tokens, :pair_w], o[tokens:, :pair_w])
-            mixed.append((o * pl.reciprocal(total, approx=True)).astype(BF16))
-        return jnp.concatenate(mixed, axis=1)
+            mix[:, lanes_of(pair)] = (o * pl.reciprocal(total, approx=True)).astype(BF16)
+            return carry
+
+        lax.fori_loop(0, pairs, one_pair, 0)
 
     low_keys = iota((half, 2 * nk), 1) < nk
 
-    def item_mix(query):
-        blocks = []
-        for f in range(feats):
-            mixed = []
-            for pair in range(pairs):
-                lanes = slice(pair * pair_w, (pair + 1) * pair_w)
-                s = dot_t(query[f * half : (f + 1) * half, lanes], k_stack[f, pair]) + item_bias[...]
+    def item_mix():
+        def one_pair(pair, carry):
+            for f in range(feats):
+                span = slice(f * half, (f + 1) * half)
+                s = dot_t(query[span, lanes_of(pair)], k_stack[f, pair]) + item_bias[...]
                 low = jnp.max(jnp.where(low_keys, s, -jnp.inf), axis=-1, keepdims=True)
                 high = jnp.max(jnp.where(low_keys, -jnp.inf, s), axis=-1, keepdims=True)
                 p = jnp.exp2(s - jnp.where(low_keys, low, high)).astype(BF16)
                 o = dot(p, v_stack[f, pair])
-                mixed.append((o[:, :pair_w] * pl.reciprocal(o[:, pair_w:], approx=True)).astype(BF16))
-            blocks.append(jnp.concatenate(mixed, axis=1))
-        return jnp.concatenate(blocks, axis=0)
+                mix[span, lanes_of(pair)] = (o[:, :pair_w] * pl.reciprocal(o[:, pair_w:], approx=True)).astype(BF16)
+            return carry
+
+        lax.fori_loop(0, pairs, one_pair, 0)
 
     @pl.when(receives)
     def _():
@@ -277,19 +288,25 @@
 
         h = h_buf[m].astype(F32)
         a = normed(h, gains_ref[0, 0:1, :])
-        q = dot(a, wqkv[:, :width]) * factor
-        k = dot(a, wqkv[:, width : 2 * width]).astype(BF16)
-        v = dot(a, wqkv[:, 2 * width :]).astype(BF16)
-        h1 = h + dot(feature_mix(q, k, v), wout[...])
+        def project(part, carry):
+            columns = pl.ds(pl.multiple_of(part * width, width), width)
+            qkv[:, columns] = dot(a, wqkv[:, columns])
+            return carry
+
+        lax.fori_loop(0, 3, project, 0)
+        feature_mix()
+        h1 = h + dot(mix[...], wout[...])
+        h1_buf[...] = h1
         b = normed(h1, gains_ref[0, 1:2, :])
-        query = (dot(b, wquery[...]) * factor).astype(BF16)
+        query[...] = (dot(b, wquery[...]) * factor).astype(BF16)
 
         @pl.when(first & (m == 0))
         def _():
             pass_cache()
             stack_cache()
 
-        result = h1 + dot(item_mix(query), witem[...])
+        item_mix()
+        result = h1_buf[...] + dot(mix[...], witem[...])
         h_out[m] = result.astype(BF16)
 
         @pl.when(sends)
@@ -326,20 +343,8 @@
         cache_pass(off, feat).wait_send()
 
 
-def hand_over(source, target, sem):
-    micro, parts = sem.shape
-    piece = source.shape[2] // parts
-    copies = []
-    for m in range(micro):
-        for part in range(parts):
-            span = pl.ds(part * piece, piece)
-            copies.append(
-                pltpu.make_async_copy(source.at[0, m, span], target.at[0, m, span], sem.at[m, part])
-            )
-    for copy in copies:
-        copy.start()
-    for copy in copies:
-        copy.wait()
+def hand_over(source, target):
+    target[...] = source[...]
 
 
 def per_device(sizes, test_rows, train_cache, pattern, feat_qkv, feat_out, item_query, item_out, gains):
@@ -382,6 +387,10 @@
             pltpu.VMEM((micro, feats, rows_n * per_row, pair_w), BF16),
             pltpu.VMEM((test_n * per_row, pair_w), F32),
             pltpu.VMEM((row_devs * train_dev * per_row, pair_w), F32),
+            pltpu.VMEM((tokens, 3 * width), F32),
+            pltpu.VMEM((tokens, width), BF16),
+            pltpu.VMEM((tokens, width), BF16),
+            pltpu.VMEM((tokens, width), F32),
             dma((4,)),
             dma((micro,)),
             dma(()),
@@ -404,9 +413,8 @@
     hidden = pl.pallas_call(
         hand_over,
         out_shape=jax.ShapeDtypeStruct(hidden.shape, hidden.dtype),
-        in_specs=[anywhere],
-        out_specs=anywhere,
-        scratch_shapes=[dma((micro, 4))],
+        in_specs=[vmem],
+        out_specs=vmem,
         compiler_params=pltpu.CompilerParams(vmem_limit_bytes=60 * 1024 * 1024),
     )(hidden)
     hidden = hidden.reshape(1, micro, test_n, pairs, gd, pair_w).swapaxes(-3, -2)

time: 41.2 us -> 37.8 us (0.917)
  Pallas kernels: 41 us -> 37.6 us
    pallas_call x1, Pallas kernels: 13.1 us -> 1.77 us  [per_device(): pl.pallas_call(hand_over, out_shape=jax.ShapeDtypeStruct(hidden.shape, hi...]
    pallas_call x1, Pallas kernels: 27.8 us -> 35.8 us  [per_device(): pl.pallas_call(functools.partial(kernel, sizes), out_shape=jax.ShapeDtype...]
where the time goes in v6:
time: 37.8 us; the launch traced here: 37.6 us
  Pallas kernels  37.6 us (99%)
    pallas_call x1, Pallas kernels, per_device(): pl.pallas_call(functools.partial(kernel, sizes), out_shape=jax.ShapeDtype...  35.8 us
    pallas_call x1, Pallas kernels, per_device(): pl.pallas_call(hand_over, out_shape=jax.ShapeDtypeStruct(hidden.shape, hi...  1.77 us

profile of v6, /device:TPU:3, one launch (start us, length us, event | category | flops | bytes accessed | tf_op | source)
XLA Modules:
  0.0 37.6 jit_solution(17015629363885937733)
XLA Ops:
  0.0 35.8 %shard_map.82.source = bf16[1,3,512,128]{3,2,1,0:T(8,128)(2,1)} custom-call(bf16[3,512,128]{2,1,0:T(8,128)(2,1)} %bitcast.15, bf16[1,2,64,128]{3,2,1,0:T(8,128)(2,1)} %bitcast.16, s32[8,8]{1,0:T(8,128)} %pattern_ref.1, bf16[1,512,1536]{2,1,0:T(8,128)(2,1)} %qkv_hbm.1, bf16[1,512,512]{2,1,0:T(8,128)(2,1)} %out_hbm.1, bf16[1,512,512]{2,1,0:T(8,128)(2,1)} %query_hbm.1, ...), custom_call_target="tpu_custom_call" | custom-call | tf_op jit(solution)/shard_map/pallas_call | solution.py:369
  35.8 1.8 %shard_map.83 = bf16[1,3,512,128]{3,2,1,0:T(8,128)(2,1)} custom-call(bf16[1,3,512,128]{3,2,1,0:T(8,128)(2,1)} %shard_map.82.source), custom_call_target="tpu_custom_call" | custom-call | tf_op jit(solution)/shard_map/pallas_call | solution.py:413

commit v7 on v5

--- a/solution.py
+++ b/solution.py
@@ -13,6 +13,8 @@
 F32 = jnp.float32
 BF16 = jnp.bfloat16
 EXCLUDED = -1e30
+SUB = 8
+VMEM_GRANT = 60 * 1024 * 1024
 
 
 def iota(shape, dim):
@@ -49,6 +51,9 @@
     per_row = gd * pairs
     train_n = cache_wide.shape[0] // per_row
     nk = train_n * gd
+    blocks = rows_n // SUB
+    block_t = tokens // blocks
+    span_t = gd * SUB
     factor = math.log2(math.e) / math.sqrt(width // HEADS)
 
     section = lax.axis_index("section")
@@ -77,8 +82,7 @@
         for m in range(micro):
             x_own(m).start()
 
-    for copy in weights:
-        copy.start()
+    weights[0].start()
     own_cache = pltpu.make_async_copy(cache_hbm.at[0], cache_buf.at[feat, row], own_sem)
     own_cache.start()
 
@@ -145,6 +149,8 @@
             x_copy(m, feat).start()
 
     cache_pass(0, feat).start()
+    for copy in weights[1:]:
+        copy.start()
 
     def h_copy(m, target):
         return pltpu.make_async_remote_copy(
@@ -164,17 +170,16 @@
         )
 
     groups = feats * gd
-    pick_q = (iota((tokens, groups), 0) // rows_n == iota((tokens, groups), 1)).astype(F32)
-    pick_k = (iota((groups, tokens), 1) // rows_n == iota((groups, tokens), 0)).astype(F32)
+    nf = block_t
+    pick_q = (iota((nf, groups), 0) // SUB == iota((nf, groups), 1)).astype(F32)
+    pick_k = ((iota((groups, 2 * nf), 1) % nf) // SUB == iota((groups, 2 * nf), 0)).astype(F32)
     pattern = (pattern_ref[...] != 0).astype(F32)
     seen = dot(dot(pick_q, pattern), pick_k) > 0.5
-    qi, ki = iota((tokens, tokens), 0), iota((tokens, tokens), 1)
-    seen = (seen | (qi == ki)) & (qi % rows_n == ki % rows_n)
-    bias = jnp.where(seen, 0.0, EXCLUDED).astype(F32)
-    feat_bias[:tokens] = bias
-    feat_bias[tokens:] = bias
+    qi, ki = iota((nf, 2 * nf), 0), iota((nf, 2 * nf), 1) % nf
+    seen = (seen | (qi == ki)) & (qi % SUB == ki % SUB)
+    feat_bias[...] = jnp.where(seen, 0.0, EXCLUDED).astype(F32)
     item_bias[...] = jnp.where(
-        iota((half, 2 * nk), 0) // rows_n == (iota((half, 2 * nk), 1) % nk) // train_n, 0.0, EXCLUDED
+        (iota((half, 2 * nk), 0) % span_t) // SUB == (iota((half, 2 * nk), 1) % nk) // train_n, 0.0, EXCLUDED
     ).astype(F32)
 
     def pass_cache():
@@ -208,40 +213,49 @@
                         v_stack[f, pair, nk:, pair_w:] = other
 
     low_half = iota((tokens, pair_w), 1) < pair_w // 2
-    ones = jnp.ones((tokens, pair_w), BF16)
+    low_ones = jnp.where(low_half[:nf], 1.0, 0.0).astype(BF16)
+    high_ones = jnp.where(low_half[:nf], 0.0, 1.0).astype(BF16)
+    ones = jnp.concatenate([low_ones, high_ones], axis=0)
+
+    def attend(s, values, n):
+        first_keys = iota(s.shape, 1) < n
+        low = jnp.max(jnp.where(first_keys, s, -jnp.inf), axis=-1, keepdims=True)
+        high = jnp.max(jnp.where(first_keys, -jnp.inf, s), axis=-1, keepdims=True)
+        p = jnp.exp2(s - jnp.where(first_keys, low, high)).astype(BF16)
+        o = dot(p, values)
+        return (o[:, :pair_w] * pl.reciprocal(o[:, pair_w:], approx=True)).astype(BF16)
 
     def feature_mix(q, k, v):
         mixed = []
         for pair in range(pairs):
             lanes = slice(pair * pair_w, (pair + 1) * pair_w)
-            q1 = q[:, lanes]
-            q2 = jnp.concatenate(
-                [jnp.where(low_half, q1, 0.0).astype(BF16), jnp.where(low_half, 0.0, q1).astype(BF16)], axis=0
-            )
-            s = dot_t(q2, k[:, lanes]) + feat_bias[...]
-            p = jnp.exp2(s - jnp.max(s, axis=-1, keepdims=True)).astype(BF16)
-            o = dot(p, jnp.concatenate([v[:, lanes], ones], axis=1))
-            total = jnp.where(low_half, o[:tokens, pair_w:], o[tokens:, pair_w:])
-            o = jnp.where(low_half, o[:tokens, :pair_w], o[tokens:, :pair_w])
-            mixed.append((o * pl.reciprocal(total, approx=True)).astype(BF16))
+            k_low = jnp.where(low_half, k[:, lanes], 0.0).astype(BF16)
+            k_high = jnp.where(low_half, 0.0, k[:, lanes]).astype(BF16)
+            v_low = jnp.where(low_half, v[:, lanes], 0.0).astype(BF16)
+            v_high = jnp.where(low_half, 0.0, v[:, lanes]).astype(BF16)
+            parts = []
+            for block in range(blocks):
+                at = slice(block * nf, (block + 1) * nf)
+                keys = jnp.concatenate([k_low[at], k_high[at]], axis=0)
+                values = jnp.concatenate([v_low[at], v_high[at]], axis=0)
+                s = dot_t(q[at, lanes], keys) + feat_bias[...]
+                parts.append(attend(s, jnp.concatenate([values, ones], axis=1), nf))
+            mixed.append(jnp.concatenate(parts, axis=0))
         return jnp.concatenate(mixed, axis=1)
 
-    low_keys = iota((half, 2 * nk), 1) < nk
-
     def item_mix(query):
-        blocks = []
+        pieces = [[None] * feats for _ in range(blocks)]
         for f in range(feats):
+            at = [slice((b * feats + f) * span_t, (b * feats + f + 1) * span_t) for b in range(blocks)]
             mixed = []
             for pair in range(pairs):
                 lanes = slice(pair * pair_w, (pair + 1) * pair_w)
-                s = dot_t(query[f * half : (f + 1) * half, lanes], k_stack[f, pair]) + item_bias[...]
-                low = jnp.max(jnp.where(low_keys, s, -jnp.inf), axis=-1, keepdims=True)
-                high = jnp.max(jnp.where(low_keys, -jnp.inf, s), axis=-1, keepdims=True)
-                p = jnp.exp2(s - jnp.where(low_keys, low, high)).astype(BF16)
-                o = dot(p, v_stack[f, pair])
-                mixed.append((o[:, :pair_w] * pl.reciprocal(o[:, pair_w:], approx=True)).astype(BF16))
-            blocks.append(jnp.concatenate(mixed, axis=1))
-        return jnp.concatenate(blocks, axis=0)
+                q = jnp.concatenate([query[span, lanes] for span in at], axis=0)
+                mixed.append(attend(dot_t(q, k_stack[f, pair]) + item_bias[...], v_stack[f, pair], nk))
+            mixed = jnp.concatenate(mixed, axis=1)
+            for b in range(blocks):
+                pieces[b][f] = mixed[b * span_t : (b + 1) * span_t]
+        return jnp.concatenate([piece for row_pieces in pieces for piece in row_pieces], axis=0)
 
     @pl.when(receives)
     def _():
@@ -249,13 +263,11 @@
         stack_cache()
 
     weights[0].wait()
-    weights[1].wait()
-    weights[2].wait()
-    weights[3].wait()
 
     def spread(pair):
         return [
-            pl.ds(f * block_n + pair * gd + g, rows_n, stride=per_row)
+            pl.ds(f * block_n + b * SUB * per_row + pair * gd + g, SUB, stride=per_row)
+            for b in range(blocks)
             for f in range(feats)
             for g in range(gd)
         ]
@@ -277,9 +289,15 @@
 
         h = h_buf[m].astype(F32)
         a = normed(h, gains_ref[0, 0:1, :])
-        q = dot(a, wqkv[:, :width]) * factor
-        k = dot(a, wqkv[:, width : 2 * width]).astype(BF16)
-        v = dot(a, wqkv[:, 2 * width :]).astype(BF16)
+        q = (dot(a, wqkv[:, :width]) * factor).astype(BF16)
+        k = dot(a, wqkv[:, width : 2 * width])
+        v = dot(a, wqkv[:, 2 * width :])
+
+        @pl.when(m == 0)
+        def _():
+            for copy in weights[1:]:
+                copy.wait()
+
         h1 = h + dot(feature_mix(q, k, v), wout[...])
         b = normed(h1, gains_ref[0, 1:2, :])
         query = (dot(b, wquery[...]) * factor).astype(BF16)
@@ -298,7 +316,7 @@
 
         for pair in range(pairs):
             for at, place in enumerate(spread(pair)):
-                wide[place, :] = result[at * rows_n : (at + 1) * rows_n, pair * pair_w : (pair + 1) * pair_w]
+                wide[place, :] = result[at * SUB : (at + 1) * SUB, pair * pair_w : (pair + 1) * pair_w]
         staged[m] = wide[...].reshape(feats, block_n, pair_w).astype(BF16)
         out_copy(m, mine).start()
         out_own(m).start()
@@ -324,22 +342,6 @@
         cache_copy(off).wait_send()
     for off in range(row_devs):
         cache_pass(off, feat).wait_send()
-
-
-def hand_over(source, target, sem):
-    micro, parts = sem.shape
-    piece = source.shape[2] // parts
-    copies = []
-    for m in range(micro):
-        for part in range(parts):
-            span = pl.ds(part * piece, piece)
-            copies.append(
-                pltpu.make_async_copy(source.at[0, m, span], target.at[0, m, span], sem.at[m, part])
-            )
-    for copy in copies:
-        copy.start()
-    for copy in copies:
-        copy.wait()
 
 
 def per_device(sizes, test_rows, train_cache, pattern, feat_qkv, feat_out, item_query, item_out, gains):
@@ -377,7 +379,7 @@
             pltpu.VMEM((feats, row_devs, 2, train_dev * per_row, pair_w), BF16),
             pltpu.VMEM((feats, pairs, 2 * nk, pair_w), BF16),
             pltpu.VMEM((feats, pairs, 2 * nk, 2 * pair_w), BF16),
-            pltpu.VMEM((2 * tokens, tokens), F32),
+            pltpu.VMEM((SUB * gd * feats, 2 * SUB * gd * feats), F32),
             pltpu.VMEM((tokens // feats, 2 * nk), F32),
             pltpu.VMEM((micro, feats, rows_n * per_row, pair_w), BF16),
             pltpu.VMEM((test_n * per_row, pair_w), F32),
@@ -398,17 +400,9 @@
             dma((micro,)),
         ],
         compiler_params=pltpu.CompilerParams(
-            collective_id=0, has_side_effects=True, vmem_limit_bytes=60 * 1024 * 1024
+            collective_id=0, has_side_effects=True, vmem_limit_bytes=VMEM_GRANT
         ),
     )(as_rows(test_rows), as_rows(train_cache), pattern, feat_qkv, feat_out, item_query, item_out, gains)
-    hidden = pl.pallas_call(
-        hand_over,
-        out_shape=jax.ShapeDtypeStruct(hidden.shape, hidden.dtype),
-        in_specs=[anywhere],
-        out_specs=anywhere,
-        scratch_shapes=[dma((micro, 4))],
-        compiler_params=pltpu.CompilerParams(vmem_limit_bytes=60 * 1024 * 1024),
-    )(hidden)
     hidden = hidden.reshape(1, micro, test_n, pairs, gd, pair_w).swapaxes(-3, -2)
     return hidden.reshape(1, micro, test_n, gd, width)
 

time: 41.2 us -> 34 us (0.83)
  Pallas kernels: 41 us -> 31.9 us
  local copies, waits for them, and re-layouts: 0 us -> 1.88 us
    pallas_call x1 -> x0, Pallas kernels: 13.1 us -> none  [per_device(): pl.pallas_call(hand_over, out_shape=jax.ShapeDtypeStruct(hidden.shape, hi...]
    pallas_call x1, Pallas kernels: 27.8 us -> 31.9 us  [per_device(): pl.pallas_call(functools.partial(kernel, sizes), out_shape=jax.ShapeDtype...]
    unnamed x0 -> x1, local copies, waits for them, and re-layouts: none -> 1.88 us
where the time goes in v7:
time: 34 us; the launch traced here: 33.8 us
  Pallas kernels  31.9 us (94%)
  local copies, waits for them, and re-layouts  1.88 us (6%)
    pallas_call x1, Pallas kernels, per_device(): pl.pallas_call(functools.partial(kernel, sizes), out_shape=jax.ShapeDtype...  31.9 us
    unnamed x1, local copies, waits for them, and re-layouts  1.88 us

profile of v7, /device:TPU:3, one launch (start us, length us, event | category | flops | bytes accessed | tf_op | source)
XLA Modules:
  0.0 33.8 jit_solution(7398139007741127059)
XLA Ops:
  0.0 31.9 %shard_map.82 = bf16[1,3,512,128]{3,2,1,0:T(8,128)(2,1)} custom-call(bf16[3,512,128]{2,1,0:T(8,128)(2,1)} %bitcast.16, bf16[1,2,64,128]{3,2,1,0:T(8,128)(2,1)} %bitcast.17, s32[8,8]{1,0:T(8,128)} %pattern_ref.1, bf16[1,512,1536]{2,1,0:T(8,128)(2,1)} %qkv_hbm.1, bf16[1,512,512]{2,1,0:T(8,128)(2,1)} %out_hbm.1, bf16[1,512,512]{2,1,0:T(8,128)(2,1)} %query_hbm.1, ...), custom_call_target="tpu_custom_call" | custom-call | tf_op jit(solution)/shard_map/pallas_call | solution.py:366
  31.9 1.9 %copy.13 = bf16[1,3,32,4,512]{4,3,2,1,0:T(4,128)(2,1)} copy(bf16[1,3,32,4,512]{4,3,2,1,0:T(4,128)(2,1)} %bitcast.15) | data formatting | bytes 786432

commit v8 on v5

--- a/solution.py
+++ b/solution.py
@@ -13,6 +13,7 @@
 F32 = jnp.float32
 BF16 = jnp.bfloat16
 EXCLUDED = -1e30
+VMEM_GRANT = 60 * 1024 * 1024
 
 
 def iota(shape, dim):
@@ -77,8 +78,7 @@
         for m in range(micro):
             x_own(m).start()
 
-    for copy in weights:
-        copy.start()
+    weights[0].start()
     own_cache = pltpu.make_async_copy(cache_hbm.at[0], cache_buf.at[feat, row], own_sem)
     own_cache.start()
 
@@ -145,6 +145,8 @@
             x_copy(m, feat).start()
 
     cache_pass(0, feat).start()
+    for copy in weights[1:]:
+        copy.start()
 
     def h_copy(m, target):
         return pltpu.make_async_remote_copy(
@@ -208,19 +210,24 @@
                         v_stack[f, pair, nk:, pair_w:] = other
 
     low_half = iota((tokens, pair_w), 1) < pair_w // 2
+    low_lanes = iota((tokens, width), 1) % pair_w < pair_w // 2
     ones = jnp.ones((tokens, pair_w), BF16)
 
+    tiles = [slice(pair * pair_w, (pair + 1) * pair_w) for pair in range(pairs)]
+
     def feature_mix(q, k, v):
+        low = jnp.where(low_lanes, q, 0.0).astype(BF16)
+        high = jnp.where(low_lanes, 0.0, q).astype(BF16)
+        queries = [jnp.concatenate([low[:, lanes], high[:, lanes]], axis=0) for lanes in tiles]
+        scores = [dot_t(q2, k[:, lanes]) for q2, lanes in zip(queries, tiles)]
+        scores = [s + feat_bias[...] for s in scores]
+        tops = [jnp.max(s, axis=-1, keepdims=True) for s in scores]
+        weights_of = [jnp.exp2(s - top).astype(BF16) for s, top in zip(scores, tops)]
+        sums = [
+            dot(p, jnp.concatenate([v[:, lanes], ones], axis=1)) for p, lanes in zip(weights_of, tiles)
+        ]
         mixed = []
-        for pair in range(pairs):
-            lanes = slice(pair * pair_w, (pair + 1) * pair_w)
-            q1 = q[:, lanes]
-            q2 = jnp.concatenate(
-                [jnp.where(low_half, q1, 0.0).astype(BF16), jnp.where(low_half, 0.0, q1).astype(BF16)], axis=0
-            )
-            s = dot_t(q2, k[:, lanes]) + feat_bias[...]
-            p = jnp.exp2(s - jnp.max(s, axis=-1, keepdims=True)).astype(BF16)
-            o = dot(p, jnp.concatenate([v[:, lanes], ones], axis=1))
+        for o in sums:
             total = jnp.where(low_half, o[:tokens, pair_w:], o[tokens:, pair_w:])
             o = jnp.where(low_half, o[:tokens, :pair_w], o[tokens:, :pair_w])
             mixed.append((o * pl.reciprocal(total, approx=True)).astype(BF16))
@@ -229,18 +236,20 @@
     low_keys = iota((half, 2 * nk), 1) < nk
 
     def item_mix(query):
-        blocks = []
-        for f in range(feats):
-            mixed = []
-            for pair in range(pairs):
-                lanes = slice(pair * pair_w, (pair + 1) * pair_w)
-                s = dot_t(query[f * half : (f + 1) * half, lanes], k_stack[f, pair]) + item_bias[...]
-                low = jnp.max(jnp.where(low_keys, s, -jnp.inf), axis=-1, keepdims=True)
-                high = jnp.max(jnp.where(low_keys, -jnp.inf, s), axis=-1, keepdims=True)
-                p = jnp.exp2(s - jnp.where(low_keys, low, high)).astype(BF16)
-                o = dot(p, v_stack[f, pair])
-                mixed.append((o[:, :pair_w] * pl.reciprocal(o[:, pair_w:], approx=True)).astype(BF16))
-            blocks.append(jnp.concatenate(mixed, axis=1))
+        units = [(f, pair) for f in range(feats) for pair in range(pairs)]
+        scores = [
+            dot_t(query[f * half : (f + 1) * half, tiles[pair]], k_stack[f, pair]) for f, pair in units
+        ]
+        scores = [s + item_bias[...] for s in scores]
+        lows = [jnp.max(jnp.where(low_keys, s, -jnp.inf), axis=-1, keepdims=True) for s in scores]
+        highs = [jnp.max(jnp.where(low_keys, -jnp.inf, s), axis=-1, keepdims=True) for s in scores]
+        weights_of = [
+            jnp.exp2(s - jnp.where(low_keys, low, high)).astype(BF16)
+            for s, low, high in zip(scores, lows, highs)
+        ]
+        sums = [dot(p, v_stack[f, pair]) for p, (f, pair) in zip(weights_of, units)]
+        mixed = [(o[:, :pair_w] * pl.reciprocal(o[:, pair_w:], approx=True)).astype(BF16) for o in sums]
+        blocks = [jnp.concatenate(mixed[f * pairs : (f + 1) * pairs], axis=1) for f in range(feats)]
         return jnp.concatenate(blocks, axis=0)
 
     @pl.when(receives)
@@ -249,9 +258,6 @@
         stack_cache()
 
     weights[0].wait()
-    weights[1].wait()
-    weights[2].wait()
-    weights[3].wait()
 
     def spread(pair):
         return [
@@ -280,6 +286,12 @@
         q = dot(a, wqkv[:, :width]) * factor
         k = dot(a, wqkv[:, width : 2 * width]).astype(BF16)
         v = dot(a, wqkv[:, 2 * width :]).astype(BF16)
+
+        @pl.when(m == 0)
+        def _():
+            for copy in weights[1:]:
+                copy.wait()
+
         h1 = h + dot(feature_mix(q, k, v), wout[...])
         b = normed(h1, gains_ref[0, 1:2, :])
         query = (dot(b, wquery[...]) * factor).astype(BF16)
@@ -324,22 +336,6 @@
         cache_copy(off).wait_send()
     for off in range(row_devs):
         cache_pass(off, feat).wait_send()
-
-
-def hand_over(source, target, sem):
-    micro, parts = sem.shape
-    piece = source.shape[2] // parts
-    copies = []
-    for m in range(micro):
-        for part in range(parts):
-            span = pl.ds(part * piece, piece)
-            copies.append(
-                pltpu.make_async_copy(source.at[0, m, span], target.at[0, m, span], sem.at[m, part])
-            )
-    for copy in copies:
-        copy.start()
-    for copy in copies:
-        copy.wait()
 
 
 def per_device(sizes, test_rows, train_cache, pattern, feat_qkv, feat_out, item_query, item_out, gains):
@@ -398,17 +394,9 @@
             dma((micro,)),
         ],
         compiler_params=pltpu.CompilerParams(
-            collective_id=0, has_side_effects=True, vmem_limit_bytes=60 * 1024 * 1024
+            collective_id=0, has_side_effects=True, vmem_limit_bytes=VMEM_GRANT
         ),
     )(as_rows(test_rows), as_rows(train_cache), pattern, feat_qkv, feat_out, item_query, item_out, gains)
-    hidden = pl.pallas_call(
-        hand_over,
-        out_shape=jax.ShapeDtypeStruct(hidden.shape, hidden.dtype),
-        in_specs=[anywhere],
-        out_specs=anywhere,
-        scratch_shapes=[dma((micro, 4))],
-        compiler_params=pltpu.CompilerParams(vmem_limit_bytes=60 * 1024 * 1024),
-    )(hidden)
     hidden = hidden.reshape(1, micro, test_n, pairs, gd, pair_w).swapaxes(-3, -2)
     return hidden.reshape(1, micro, test_n, gd, width)
 

time: 41.2 us -> 25.4 us (0.62)
  Pallas kernels: 41 us -> 23.3 us
  local copies, waits for them, and re-layouts: 0 us -> 1.88 us
    pallas_call x1 -> x0, Pallas kernels: 13.1 us -> none  [per_device(): pl.pallas_call(hand_over, out_shape=jax.ShapeDtypeStruct(hidden.shape, hi...]
    pallas_call x1, Pallas kernels: 27.8 us -> 23.3 us  [per_device(): pl.pallas_call(functools.partial(kernel, sizes), out_shape=jax.ShapeDtype...]
    unnamed x0 -> x1, local copies, waits for them, and re-layouts: none -> 1.88 us
where the time goes in v8:
time: 25.4 us; the launch traced here: 25.2 us
  Pallas kernels  23.3 us (92%)
  local copies, waits for them, and re-layouts  1.88 us (7%)
    pallas_call x1, Pallas kernels, per_device(): pl.pallas_call(functools.partial(kernel, sizes), out_shape=jax.ShapeDtype...  23.3 us
    unnamed x1, local copies, waits for them, and re-layouts  1.88 us

profile of v8, /device:TPU:3, one launch (start us, length us, event | category | flops | bytes accessed | tf_op | source)
XLA Modules:
  0.0 25.2 jit_solution(2887444490145616200)
XLA Ops:
  0.0 23.3 %shard_map.82 = bf16[1,3,512,128]{3,2,1,0:T(8,128)(2,1)} custom-call(bf16[3,512,128]{2,1,0:T(8,128)(2,1)} %bitcast.16, bf16[1,2,64,128]{3,2,1,0:T(8,128)(2,1)} %bitcast.17, s32[8,8]{1,0:T(8,128)} %pattern_ref.1, bf16[1,512,1536]{2,1,0:T(8,128)(2,1)} %qkv_hbm.1, bf16[1,512,512]{2,1,0:T(8,128)(2,1)} %out_hbm.1, bf16[1,512,512]{2,1,0:T(8,128)(2,1)} %query_hbm.1, ...), custom_call_target="tpu_custom_call" | custom-call | tf_op jit(solution)/shard_map/pallas_call | solution.py:360
  23.3 1.9 %copy.13 = bf16[1,3,32,4,512]{4,3,2,1,0:T(4,128)(2,1)} copy(bf16[1,3,32,4,512]{4,3,2,1,0:T(4,128)(2,1)} %bitcast.15) | data formatting | bytes 786432

commit v9 on v8

--- a/solution.py
+++ b/solution.py
@@ -215,11 +215,12 @@
 
     tiles = [slice(pair * pair_w, (pair + 1) * pair_w) for pair in range(pairs)]
 
-    def feature_mix(q, k, v):
+    def feature_mix(a, q, k):
         low = jnp.where(low_lanes, q, 0.0).astype(BF16)
         high = jnp.where(low_lanes, 0.0, q).astype(BF16)
         queries = [jnp.concatenate([low[:, lanes], high[:, lanes]], axis=0) for lanes in tiles]
         scores = [dot_t(q2, k[:, lanes]) for q2, lanes in zip(queries, tiles)]
+        v = dot(a, wqkv[:, 2 * width :]).astype(BF16)
         scores = [s + feat_bias[...] for s in scores]
         tops = [jnp.max(s, axis=-1, keepdims=True) for s in scores]
         weights_of = [jnp.exp2(s - top).astype(BF16) for s, top in zip(scores, tops)]
@@ -281,18 +282,16 @@
         def _():
             h_copy(m, section - 1).wait_recv()
 
+        @pl.when(m == 0)
+        def _():
+            for copy in weights[1:]:
+                copy.wait()
+
         h = h_buf[m].astype(F32)
         a = normed(h, gains_ref[0, 0:1, :])
         q = dot(a, wqkv[:, :width]) * factor
         k = dot(a, wqkv[:, width : 2 * width]).astype(BF16)
-        v = dot(a, wqkv[:, 2 * width :]).astype(BF16)
-
-        @pl.when(m == 0)
-        def _():
-            for copy in weights[1:]:
-                copy.wait()
-
-        h1 = h + dot(feature_mix(q, k, v), wout[...])
+        h1 = h + dot(feature_mix(a, q, k), wout[...])
         b = normed(h1, gains_ref[0, 1:2, :])
         query = (dot(b, wquery[...]) * factor).astype(BF16)
 

time: 25.4 us -> 25.1 us (0.988)
  Pallas kernels: 23.3 us -> 23 us
where the time goes in v9:
time: 25.1 us; the launch traced here: 24.9 us
  Pallas kernels  23 us (92%)
  local copies, waits for them, and re-layouts  1.88 us (7%)
    pallas_call x1, Pallas kernels, per_device(): pl.pallas_call(functools.partial(kernel, sizes), out_shape=jax.ShapeDtype...  23 us
    unnamed x1, local copies, waits for them, and re-layouts  1.88 us

profile of v9, /device:TPU:3, one launch (start us, length us, event | category | flops | bytes accessed | tf_op | source)
XLA Modules:
  0.0 24.9 jit_solution(4512117611510646833)
XLA Ops:
  0.0 23.0 %shard_map.82 = bf16[1,3,512,128]{3,2,1,0:T(8,128)(2,1)} custom-call(bf16[3,512,128]{2,1,0:T(8,128)(2,1)} %bitcast.16, bf16[1,2,64,128]{3,2,1,0:T(8,128)(2,1)} %bitcast.17, s32[8,8]{1,0:T(8,128)} %pattern_ref.1, bf16[1,512,1536]{2,1,0:T(8,128)(2,1)} %qkv_hbm.1, bf16[1,512,512]{2,1,0:T(8,128)(2,1)} %out_hbm.1, bf16[1,512,512]{2,1,0:T(8,128)(2,1)} %query_hbm.1, ...), custom_call_target="tpu_custom_call" | custom-call | tf_op jit(solution)/shard_map/pallas_call | solution.py:359
  23.1 1.9 %copy.13 = bf16[1,3,32,4,512]{4,3,2,1,0:T(4,128)(2,1)} copy(bf16[1,3,32,4,512]{4,3,2,1,0:T(4,128)(2,1)} %bitcast.15) | data formatting | bytes 786432
